TPU v7x, 32 devices: a whole 2x2x4 slice. The times are simulated.
32 devices in a mesh: fsdp: 8 (over z, y), rep: 4 (over x, core).
Axes of the slice: x: 2, y: 2, z: 4, core: 2. Of those that a mesh axis runs over, the one named last changes fastest.
Arguments:
- tokens: bfloat16 [2, 4096, 2048], P(None, ('fsdp', 'rep')), may hold values from -6 to 6
- segment_ids: int32 [2, 32, 128], P(None, ('fsdp', 'rep')), may hold values from 0 to 2, never falling along the last dimension, each value on 1 to 64 neighbouring positions
- out_grad: bfloat16 [2, 4096, 2048], P(None, ('fsdp', 'rep')), may hold values from -6 to 6
- norm_gain: bfloat16 [2048], P('fsdp'), may hold values from 0.25 to 1.75
- in_proj: bfloat16 [2048, 8192], P('fsdp'), may hold values from -0.125 to 0.125
- conv_weight: bfloat16 [4096, 4], P('fsdp'), may hold values from -3 to 3
- conv_bias: bfloat16 [4096], P('fsdp'), may hold values from -3 to 3
- x_proj: bfloat16 [4096, 160], P('fsdp'), may hold values from -0.09375 to 0.09375
- step_proj: bfloat16 [4096, 128], P('fsdp'), may hold values from -0.5 to 0.5
- step_bias: bfloat16 [4096], P('fsdp'), may hold values from -4 to -1
- decay_log: bfloat16 [4096, 16], P('fsdp'), may hold values from -1 to 2.5
- skip_gain: bfloat16 [4096], P('fsdp'), may hold values from 0.5 to 1.5
- out_proj: bfloat16 [4096, 2048], P('fsdp'), may hold values from -0.375 to 0.375
Outputs:
- block_out: bfloat16 [2, 4096, 2048], P(None, ('fsdp', 'rep'))
- input_grad: bfloat16 [2, 4096, 2048], P(None, ('fsdp', 'rep'))
- gain_grad: float32 [2048], P('fsdp')
- in_proj_grad: float32 [2048, 8192], P('fsdp')
- conv_weight_grad: float32 [4096, 4], P('fsdp')
- conv_bias_grad: float32 [4096], P('fsdp')
- x_proj_grad: float32 [4096, 160], P('fsdp')
- step_proj_grad: float32 [4096, 128], P('fsdp')
- step_bias_grad: float32 [4096], P('fsdp')
- decay_log_grad: float32 [4096, 16], P('fsdp')
- skip_gain_grad: float32 [4096], P('fsdp')
- out_proj_grad: float32 [4096, 2048], P('fsdp')
Inputs may be any that keep to these rules, and one draw needn't show every extreme that they name: `segment_ids`: segment numbers never fall along a sequence; each change starts a new document.
All inputs are finite; a program needn't handle non-finite values.
Results may differ from a plain program's by a relative error of at most 0.012.
Values may be sent and summed in bfloat16 or wider, within the bound.
A program may use at most 240 MiB of HBM per device.

v0:
```python
import functools

import jax
import jax.numpy as jnp
from jax import lax
from jax.experimental import pallas as pl
from jax.experimental.pallas import tpu as pltpu
from jax.sharding import PartitionSpec as P

EPS = 1e-05
BLOCK = 16
LANES = 128
GROUP = 8
COPIES = 4
LOG2E = 1.4426950408889634
LN2 = 0.6931471805599453
FAR = 1e30
F32 = jnp.float32
BF16 = jnp.bfloat16
VMEM_LIMIT = 56 * 1024 * 1024


def dot(left, right, left_dim, right_dim):
    return lax.dot_general(
        left, right, (((left_dim,), (right_dim,)), ((), ())), preferred_element_type=F32
    )


def params():
    return pltpu.CompilerParams(vmem_limit_bytes=VMEM_LIMIT)


def cost(flops, moved):
    return pl.CostEstimate(flops=int(flops), bytes_accessed=int(moved), transcendentals=0)


def blank(shape, dtype):
    return pl.pallas_call(
        lambda ref: None,
        out_shape=jax.ShapeDtypeStruct(shape, dtype),
        out_specs=pl.BlockSpec(memory_space=pl.ANY),
        name="blank",
    )()


def ring_order(size):
    half = size // 2
    return [2 * p if p < half else 2 * (size - 1 - p) + 1 for p in range(size)]


class Ring:
    def __init__(self, size):
        order = ring_order(size)
        place = [0] * size
        for spot, member in enumerate(order):
            place[member] = spot
        self.size, self.half = size, size // 2
        self.order = jnp.array(order, jnp.int32)
        self.spot = jnp.array(place, jnp.int32)[lax.axis_index("fsdp")]
        self.above = [(order[p], order[(p + 1) % size]) for p in range(size)]
        self.below = [(order[p], order[(p - 1) % size]) for p in range(size)]

    def member(self, offset):
        return self.order[(self.spot + offset + self.size) % self.size]

    def up(self, value):
        return lax.ppermute(value, "fsdp", self.above)

    def down(self, value):
        return lax.ppermute(value, "fsdp", self.below)


class Gather:
    def __init__(self, ring, shard):
        self.ring, self.cut = ring, shard.shape[0] // 2
        self.whole = blank((ring.size,) + shard.shape, shard.dtype)
        self.held = (shard, shard)
        self.put(shard, 0)

    def put(self, piece, offset, start=0):
        at = (self.ring.member(offset), jnp.int32(start), jnp.int32(0))
        self.whole = lax.dynamic_update_slice(self.whole, piece[None], at)

    def step(self, number):
        low, high = self.held
        if number == self.ring.half:
            low, high = low[: self.cut], high[self.cut :]
        return self.ring.up(low), self.ring.down(high)

    def take(self, number, got):
        self.held = got
        last = number == self.ring.half
        self.put(got[0], -number)
        self.put(got[1], number, self.cut if last else 0)

    def rest(self):
        def body(number, state):
            whole, low, high = state
            low, high = self.ring.up(low), self.ring.down(high)
            self.whole = whole
            self.put(low, -number)
            self.put(high, number)
            return self.whole, low, high

        self.whole, low, high = lax.fori_loop(1, self.ring.half, body, (self.whole,) + self.held)
        self.held = (low, high)
        self.take(self.ring.half, self.step(self.ring.half))


class Scatter:
    def __init__(self, ring, parts):
        self.ring, self.parts, self.cut = ring, parts, parts.shape[1] // 2
        far = self.own(ring.half)
        self.sent = (far[: self.cut], far[self.cut :])
        self.total = None

    def own(self, offset):
        return lax.dynamic_index_in_dim(self.parts, self.ring.member(offset), 0, keepdims=False)

    def step(self, number):
        return self.ring.up(self.sent[0]), self.ring.down(self.sent[1])

    def take(self, number, got):
        left = self.ring.half - number
        low, high = got
        near_low, near_high = self.own(left), self.own(-left)
        if number == 1:
            low = jnp.concatenate([low, jnp.zeros_like(near_low[self.cut :])])
            high = jnp.concatenate([jnp.zeros_like(near_high[: self.cut]), high])
        if left == 0:
            self.total = near_low.astype(F32) + low.astype(F32) + high.astype(F32)
        else:
            self.sent = (self.add(near_low, low), self.add(near_high, high))

    def add(self, near, got):
        return (near.astype(F32) + got.astype(F32)).astype(near.dtype)

    def rest(self):
        self.take(1, self.step(1))

        def body(number, sent):
            left = self.ring.half - number
            low, high = self.ring.up(sent[0]), self.ring.down(sent[1])
            return self.add(self.own(left), low), self.add(self.own(-left), high)

        self.sent = lax.fori_loop(2, self.ring.half, body, self.sent)
        self.take(self.ring.half, self.step(self.ring.half))


def swap(value, bit):
    return lax.ppermute(value, "rep", [(r, r ^ bit) for r in range(COPIES)])


def rep_gather(value):
    across = swap(value, 2)
    return [value, swap(value, 1), across, swap(across, 1)]


def rep_scatter_near(parts):
    pair = swap(jnp.stack([parts[1], parts[3]]), 1)
    near = parts[0].astype(F32) + pair[0].astype(F32)
    far = parts[2].astype(F32) + pair[1].astype(F32)
    return near, far.astype(parts.dtype)


def rep_scatter_far(near, far):
    return near + swap(far, 2).astype(F32)


def sum_near(parts):
    pair = swap(jnp.stack([parts[1], parts[3]]), 1)
    mine = jnp.stack([parts[0], parts[2]]) + pair
    return mine + swap(jnp.stack([mine[1], mine[0]]), 2)


def sum_far(mine):
    next_to = swap(mine, 1)
    return jnp.stack([mine[0], next_to[0], mine[1], next_to[1]])


def to_time(value):
    return jnp.swapaxes(value.reshape(GROUP, -1, value.shape[-1]), 0, 1).reshape(value.shape)


def to_sequence(value):
    return jnp.swapaxes(value.reshape(-1, GROUP, value.shape[-1]), 0, 1).reshape(value.shape)


def by_copy(value):
    return value.reshape(COPIES, -1, value.shape[-1])


def sigmoid(value):
    return 1.0 / (1.0 + jnp.exp(-value))


def later(value, shift):
    rows = shift * GROUP
    return jnp.concatenate([jnp.zeros_like(value[:rows]), value[:-rows]], axis=0)


def sooner(value, shift):
    rows = shift * GROUP
    return jnp.concatenate([value[rows:], jnp.zeros_like(value[:rows])], axis=0)


def conv_of(inner, masks, taps):
    total = taps[4:5] + taps[3:4] * inner
    for shift in range(1, 4):
        total = total + taps[3 - shift : 4 - shift] * (later(inner, shift) * masks[shift - 1])
    return total


def by_sequence(held, out_ref, value):
    length = value.shape[0] // GROUP
    held[...] = value
    for s in range(GROUP):
        out_ref[s * length : (s + 1) * length, :] = held[
            pl.ds(s, length, stride=GROUP), :
        ].astype(out_ref.dtype)


def conv_kernel(inner_ref, masks_ref, taps_ref, act_ref, low_ref):
    value = conv_of(inner_ref[...], masks_ref, taps_ref[...])
    act = value * sigmoid(value)
    act_ref[...] = act
    low_ref[...] = act.astype(BF16)


def conv_forward(inner, masks, taps):
    rows, width = inner.shape
    tile = pl.BlockSpec((rows, LANES), lambda c: (0, c))
    return pl.pallas_call(
        conv_kernel,
        grid=(width // LANES,),
        in_specs=[
            tile,
            pl.BlockSpec((3, rows, LANES), lambda c: (0, 0, 0)),
            pl.BlockSpec((8, LANES), lambda c: (0, c)),
        ],
        out_specs=[tile, tile],
        out_shape=[
            jax.ShapeDtypeStruct((rows, width), F32),
            jax.ShapeDtypeStruct((rows, width), BF16),
        ],
        compiler_params=params(),
        cost_estimate=cost(30 * rows * width, 10 * rows * width),
        name="conv_forward",
    )(inner, masks, taps)


def conv_back_kernel(inner_ref, grad_ref, masks_ref, taps_ref, out_ref, natural_ref, sums_ref, held):
    inner, taps = inner_ref[...], taps_ref[...]
    value = conv_of(inner, masks_ref, taps)
    gate = sigmoid(value)
    grad = grad_ref[...] * (gate * (1.0 + value * (1.0 - gate)))
    total = taps[3:4] * grad
    sums = [None] * 4 + [jnp.sum(grad, axis=0, keepdims=True)]
    sums[3] = jnp.sum(grad * inner, axis=0, keepdims=True)
    for shift in range(1, 4):
        masked = grad * masks_ref[shift - 1]
        total = total + taps[3 - shift : 4 - shift] * sooner(masked, shift)
        sums[3 - shift] = jnp.sum(masked * later(inner, shift), axis=0, keepdims=True)
    out_ref[...] = total.astype(BF16)
    by_sequence(held, natural_ref, total)
    sums_ref[...] = jnp.concatenate(sums + [jnp.zeros((3, inner.shape[1]), F32)], axis=0)


def conv_backward(inner, grad, masks, taps):
    rows, width = inner.shape
    tile = pl.BlockSpec((rows, LANES), lambda c: (0, c))
    few = pl.BlockSpec((8, LANES), lambda c: (0, c))
    return pl.pallas_call(
        conv_back_kernel,
        grid=(width // LANES,),
        in_specs=[tile, tile, pl.BlockSpec((3, rows, LANES), lambda c: (0, 0, 0)), few],
        out_specs=[tile, tile, few],
        out_shape=[
            jax.ShapeDtypeStruct((rows, width), BF16),
            jax.ShapeDtypeStruct((rows, width), BF16),
            jax.ShapeDtypeStruct((8, width), F32),
        ],
        scratch_shapes=[pltpu.VMEM((rows, LANES), F32)],
        compiler_params=params(),
        cost_estimate=cost(60 * rows * width, 10 * rows * width),
        name="conv_backward",
    )(inner, grad, masks, taps)


def gate_kernel(readout_ref, gate_ref, out_ref, natural_ref, held):
    gate = gate_ref[...]
    gated = readout_ref[...] * (gate * sigmoid(gate))
    out_ref[...] = gated.astype(BF16)
    by_sequence(held, natural_ref, gated)


def gate_forward(readout, gate):
    rows, width = gate.shape
    tile = pl.BlockSpec((rows, LANES), lambda c: (0, c))
    return pl.pallas_call(
        gate_kernel,
        grid=(width // LANES,),
        in_specs=[tile] * 2,
        out_specs=[tile] * 2,
        out_shape=[jax.ShapeDtypeStruct((rows, width), BF16)] * 2,
        scratch_shapes=[pltpu.VMEM((rows, LANES), F32)],
        compiler_params=params(),
        cost_estimate=cost(20 * rows * width, 12 * rows * width),
        name="gate_forward",
    )(readout, gate)


def gate_back_kernel(grad_ref, readout_ref, gate_ref, read_ref, out_ref, natural_ref, held):
    gate, grad = gate_ref[...], grad_ref[...]
    sig = sigmoid(gate)
    read_ref[...] = grad * (gate * sig)
    gate_grad = grad * readout_ref[...] * (sig * (1.0 + gate * (1.0 - sig)))
    out_ref[...] = gate_grad.astype(BF16)
    by_sequence(held, natural_ref, gate_grad)


def gate_backward(grad, readout, gate):
    rows, width = gate.shape
    tile = pl.BlockSpec((rows, LANES), lambda c: (0, c))
    return pl.pallas_call(
        gate_back_kernel,
        grid=(width // LANES,),
        in_specs=[tile] * 3,
        out_specs=[tile] * 3,
        out_shape=[jax.ShapeDtypeStruct((rows, width), F32)]
        + [jax.ShapeDtypeStruct((rows, width), BF16)] * 2,
        scratch_shapes=[pltpu.VMEM((rows, LANES), F32)],
        compiler_params=params(),
        cost_estimate=cost(20 * rows * width, 20 * rows * width),
        name="gate_backward",
    )(grad, readout, gate)


def rows_kernel(scaled, *refs):
    values_ref, out_ref, held = refs[0], refs[-2], refs[-1]
    for s in range(GROUP):
        value = values_ref[s].astype(F32)
        if scaled:
            square = jnp.mean(value * value, axis=-1, keepdims=True)
            value = value * lax.rsqrt(square + EPS) * refs[1][...]
        for k in range(held.shape[0]):
            held[k, pl.ds(s, value.shape[0], stride=GROUP), :] = value[
                :, k * LANES : (k + 1) * LANES
            ]
    for k in range(held.shape[0]):
        out_ref[:, k * LANES : (k + 1) * LANES] = held[k].astype(BF16)


def interleave(values, gain=None):
    _, length, model = values.shape
    extra = [] if gain is None else [gain.reshape(1, model)]
    return pl.pallas_call(
        functools.partial(rows_kernel, gain is not None),
        grid=(length // BLOCK,),
        in_specs=[pl.BlockSpec((GROUP, BLOCK, model), lambda t: (0, t, 0))]
        + [pl.BlockSpec((1, model), lambda t: (0, 0))] * len(extra),
        out_specs=pl.BlockSpec((BLOCK * GROUP, model), lambda t: (t, 0)),
        out_shape=jax.ShapeDtypeStruct((length * GROUP, model), BF16),
        scratch_shapes=[pltpu.VMEM((model // LANES, BLOCK * GROUP, LANES), F32)],
        compiler_params=params(),
        cost_estimate=cost(8 * GROUP * length * model, 4 * GROUP * length * model),
        name="interleave",
    )(values, *extra)


class Peers:
    def __init__(self, size):
        self.size, self.half = size, size // 2
        self.member, self.copy = lax.axis_index("fsdp"), lax.axis_index("rep")
        row, column = lax.div(self.member, 2), lax.rem(self.member, 2)
        self.spot = row * (1 - column) + (size - 1 - row) * column
        side = lax.rem(self.copy, 2)
        self.core = (self.member, self.copy - side + (1 - side))
        self.across = (self.member, lax.rem(self.copy + 2, COPIES))
        self.ring = ((self.at(1), self.copy), (self.at(-1), self.copy))

    def at(self, offset):
        spot = lax.rem(self.spot + (offset + self.size), self.size)
        second = lax.div(spot, self.half)
        return 2 * spot * (1 - second) + (2 * (self.size - 1 - spot) + 1) * second

    def meet(self):
        barrier = pltpu.get_barrier_semaphore()
        peers = (*self.ring, self.core, self.across)
        for peer in peers:
            pl.semaphore_signal(barrier, inc=1, device_id=peer, device_id_type=pl.DeviceIdType.MESH)
        pl.semaphore_wait(barrier, len(peers))


def remote(source, target, sems, index, peer):
    return pltpu.make_async_remote_copy(
        src_ref=source,
        dst_ref=target,
        send_sem=sems[0].at[index],
        recv_sem=sems[1].at[index],
        device_id=peer,
        device_id_type=pl.DeviceIdType.MESH,
    )


def spread(coefs, nstate):
    terms = []
    for _ in range(3):
        term = coefs.astype(BF16)
        terms.append(term)
        coefs = coefs - term.astype(F32)
    joined = jnp.concatenate(terms, axis=1)
    return jnp.pad(joined, ((0, 0), (0, LANES - joined.shape[1])))


def spreader(nstate):
    row = lax.broadcasted_iota(jnp.int32, (LANES, 2 * nstate * LANES), 0)
    tile = lax.broadcasted_iota(jnp.int32, (LANES, 2 * nstate * LANES), 1) // LANES
    return ((row % (2 * nstate) == tile) & (row < 6 * nstate)).astype(BF16)


def folder(nstate):
    tile = lax.broadcasted_iota(jnp.int32, (2 * nstate * LANES, LANES), 0) // LANES
    column = lax.broadcasted_iota(jnp.int32, (2 * nstate * LANES, LANES), 1)
    return (tile == column).astype(BF16)


def tiled(value, width):
    return jnp.concatenate([value] * (width // LANES), axis=1)


def at_time(t):
    return pl.ds(pl.multiple_of(t * GROUP, GROUP), GROUP)


def scan_kernel(
    nstate, chunk, pre_ref, act_ref, coef_ref, spread_ref, keep_ref, rate_ref, row_ref,
    out_ref, step_ref, start_ref, carry_ref, wide,
):
    width = pre_ref.shape[1]

    @pl.when(pl.program_id(0) == 0)
    def _():
        carry_ref[...] = jnp.zeros_like(carry_ref)

    start_ref[0] = carry_ref[...]
    wide[...] = jnp.dot(coef_ref[...], spread_ref[...], preferred_element_type=F32)
    pre = pre_ref[...] + row_ref[0:1]
    step_ref[...] = jnp.maximum(pre, 0.0) + jnp.log1p(jnp.exp(-jnp.abs(pre)))
    for c in range(width // chunk):
        cols = slice(c * chunk, (c + 1) * chunk)

        def advance(t, states):
            at = at_time(t)
            step, act = step_ref[at, cols], act_ref[at, cols]
            drive = jnp.where(tiled(keep_ref[at, :], chunk) > 0.5, step, FAR)
            inflow = step * act
            total = row_ref[1:2, cols] * act
            now = []
            for n in range(nstate):
                write = tiled(wide[at, n * LANES : (n + 1) * LANES], chunk)
                read = tiled(wide[at, (nstate + n) * LANES : (nstate + n + 1) * LANES], chunk)
                state = jnp.exp2(drive * rate_ref[n, :, cols]) * states[n] + write * inflow
                total = total + read * state
                now.append(state)
            out_ref[at, cols] = total
            return tuple(now)

        start = tuple(carry_ref[n, :, cols] for n in range(nstate))
        states = lax.fori_loop(0, BLOCK, advance, start, unroll=4)
        for n in range(nstate):
            carry_ref[n, :, cols] = states[n]


def scan_forward(pre, act, coef, spread_by, keep, rate, rows):
    total, width = pre.shape
    nstate = rate.shape[0]
    size = BLOCK * GROUP
    tile = pl.BlockSpec((size, width), lambda t: (t, 0))
    thin = pl.BlockSpec((size, LANES), lambda t: (t, 0))
    state = pl.BlockSpec((nstate, GROUP, width), lambda t: (0, 0, 0))
    count = total // size
    work = total * width * nstate
    return pl.pallas_call(
        functools.partial(scan_kernel, nstate, 256),
        grid=(count,),
        in_specs=[
            tile,
            tile,
            thin,
            pl.BlockSpec(spread_by.shape, lambda t: (0, 0)),
            thin,
            state,
            pl.BlockSpec((8, width), lambda t: (0, 0)),
        ],
        out_specs=[
            tile,
            tile,
            pl.BlockSpec((1, nstate, GROUP, width), lambda t: (t, 0, 0, 0)),
        ],
        out_shape=[
            jax.ShapeDtypeStruct((total, width), F32),
            jax.ShapeDtypeStruct((total, width), F32),
            jax.ShapeDtypeStruct((total // size, nstate, GROUP, width), F32),
        ],
        scratch_shapes=[
            pltpu.VMEM((nstate, GROUP, width), F32),
            pltpu.VMEM((size, 2 * nstate * LANES), F32),
        ],
        compiler_params=params(),
        cost_estimate=cost(16 * work, 16 * count * size * width),
        name="scan_forward",
    )(pre, act, coef, spread_by, keep, rate, rows)


class Shares:
    def __init__(self, peers, shards, wholes, sems):
        self.peers, self.shards, self.wholes, self.sems = peers, shards, wholes, sems
        self.sent = []

    def place(self, which, member, c):
        rows = self.shards[which].shape[0]
        start = pl.multiple_of(member * rows + c * (rows // 2), rows // 2)
        return self.wholes[which].at[pl.ds(start, rows // 2), :]

    def owner(self, way, step):
        return self.peers.at(-step if way == 0 else step)

    def chunks(self, way, step):
        return (way,) if step == self.peers.half else (0, 1)

    def come(self, which, way, step, c):
        there = self.place(which, self.owner(way, step), c)
        remote(there, there, self.sems, (which, way, step - 1, c), self.peers.ring[way]).wait_recv()

    def step(self, which, step):
        for c in range(2):
            for way in range(2):
                if c not in self.chunks(way, step):
                    continue
                target = self.place(which, self.owner(way, step - 1), c)
                source = target
                if step == 1:
                    rows = self.shards[which].shape[0] // 2
                    source = self.shards[which].at[pl.ds(c * rows, rows), :]
                else:
                    self.come(which, way, step - 1, c)
                index = (which, way, step - 1, c)
                remote(source, target, self.sems, index, self.peers.ring[way]).start()

    def finish(self, which):
        half = self.peers.half
        for way in range(2):
            self.come(which, way, half - 1, 1 - way)
            self.come(which, way, half, way)

    def sent_all(self):
        for which in range(len(self.shards)):
            for step in range(1, self.peers.half + 1):
                for way in range(2):
                    for c in self.chunks(way, step):
                        place = self.place(which, self.owner(way, step - 1), c)
                        index = (which, way, step - 1, c)
                        remote(place, place, self.sems, index, self.peers.ring[way]).wait_send()


def softplus(value):
    return jnp.maximum(value, 0.0) + jnp.log1p(jnp.exp(-jnp.abs(value)))


def forward_kernel(
    size, rank, nstate,
    entry, few, tokens, out_grad, segments, out_proj,
    few_out, masks_out, rate_out, spread_out, fold_out, normed_out, cotangent_out, tokens_all, grads_all, segments_all,
    w_in_out, inner_out, act_out, low_out, step_low_out, coef_out, step_out, start_out, gate_out, readout_out,
    gated_out, natural_out, gate_w_out, out_w_out,
    few_all, small, masks, rate, spread_by, fold_by, normed, stage, cotangent, held, seg, inner_shard, gate_shard, w_in,
    inner, act, low, part, nat, got_near, to_across, got_across, shared, step_low, coef, wide, pre, step, readout,
    carry, start_at, gate, gated, natural, gate_w,
    local, start_sems, gate_sems, own_sems, entry_sems, stage_sems, out_sems, seg_sems,
    ring_send, ring_recv, few_send, few_recv, rep_send, rep_recv, near_send, near_recv,
):
    peers = Peers(size)
    total, width = normed.shape[0], w_in.shape[1]
    pad = 3 * GROUP
    chunk = 256
    rows = 64
    length = total // GROUP
    batches = GROUP // COPIES
    half = peers.half
    side_rows = total // COPIES
    saved = []

    def save(source, target):
        copy = pltpu.make_async_copy(source, target, local.at[len(saved)])
        copy.start()
        saved.append(copy)

    picks = []
    for side_of, target in enumerate((inner_shard, gate_shard)):
        for f in range(size):
            source = ((side_of * size + f) * COPIES + peers.copy) * LANES
            picks.append(
                pltpu.make_async_copy(
                    entry.at[:, pl.ds(pl.multiple_of(source, LANES), LANES)],
                    target.at[:, pl.ds(f * LANES, LANES)],
                    entry_sems.at[len(picks)],
                )
            )
    for pick in picks:
        pick.start()
    peers.meet()
    sent = []

    def send(*copy):
        moving = remote(*copy)
        moving.start()
        sent.append(moving)

    rep_sems = (rep_send, rep_recv)

    def of_copy(ref, k):
        return ref.at[k] if ref is segments_all else ref.at[pl.ds(k * batches, batches)]

    def exchange(i, own, everyone):
        send(own, of_copy(everyone, 2), rep_sems, (i, 0), peers.across)
        send(own, of_copy(everyone, 1), rep_sems, (i, 1), peers.core)
        copy = pltpu.make_async_copy(own, of_copy(everyone, 0), own_sems.at[3 + i])
        copy.start()
        return copy

    def pass_on(i, everyone):
        far = of_copy(everyone, 2)
        remote(far, far, rep_sems, (i, 0), peers.across).wait_recv()
        send(far, of_copy(everyone, 3), rep_sems, (i, 2), peers.core)

    def exchanged(i, everyone, copy):
        copy.wait()
        for k, which in ((1, 1), (3, 2)):
            there = of_copy(everyone, k)
            remote(there, there, rep_sems, (i, which), peers.core).wait_recv()

    out_rows = out_proj.shape[0] // COPIES
    out_shard = out_proj.at[pl.ds(pl.multiple_of(peers.copy * out_rows, out_rows), out_rows), :]
    ring = Shares(
        peers, (inner_shard, gate_shard, out_shard), (w_in, gate_w, out_w_out), (ring_send, ring_recv),
    )
    gate_rows = gate_shard.shape[0]
    shard_rows = pl.ds(pl.multiple_of(peers.member * gate_rows, gate_rows), gate_rows)
    own_rows = pl.ds(pl.multiple_of(peers.member * out_rows, out_rows), out_rows)
    own_columns = pl.ds(pl.multiple_of(peers.member * LANES, LANES), LANES)

    few_sems = (few_send, few_recv)
    few_rows = few.shape[0] // 2

    def few_place(way, number, split):
        columns = pl.ds(pl.multiple_of(ring.owner(way, number) * LANES, LANES), LANES)
        place = pl.ds(way * few_rows, few_rows) if split else pl.ds(0, 2 * few_rows)
        return few_all.at[place, columns]

    def few_come(way, number):
        there = few_place(way, number, number == half)
        remote(there, there, few_sems, (way, number - 1), peers.ring[way]).wait_recv()

    def few_step(number):
        for way in range(2):
            if number > 1:
                few_come(way, number - 1)
            target = few_place(way, number - 1, number == half)
            source = few if number == 1 else target
            send(source, target, few_sems, (way, number - 1), peers.ring[way])

    few_step(1)
    own_tokens = exchange(0, tokens, tokens_all)
    own_segments = exchange(2, segments, segments_all)
    own = [
        pltpu.make_async_copy(few, few_all.at[:, own_columns], own_sems.at[0]),
        pltpu.make_async_copy(out_shard, out_w_out.at[own_rows, :], own_sems.at[1]),
    ]
    for copy in own:
        copy.start()
    for pick in picks[:size]:
        pick.wait()
    ring.step(0, 1)
    for pick in picks[size:]:
        pick.wait()
    own_shards = [
        pltpu.make_async_copy(inner_shard, w_in.at[shard_rows, :], own_sems.at[6]),
        pltpu.make_async_copy(gate_shard, gate_w.at[shard_rows, :], own_sems.at[2]),
    ]
    for copy in own_shards:
        copy.start()

    wide_shape, thin_shape = spread_by.shape, fold_by.shape
    tile = lax.broadcasted_iota(jnp.int32, wide_shape, 1) // LANES
    row = lax.broadcasted_iota(jnp.int32, wide_shape, 0)
    spread_by[...] = jnp.where(
        (lax.rem(row, 2 * nstate) == tile) & (row < 6 * nstate), 1.0, 0.0
    ).astype(BF16)
    tile = lax.broadcasted_iota(jnp.int32, thin_shape, 0) // LANES
    column = lax.broadcasted_iota(jnp.int32, thin_shape, 1)
    fold_by[...] = jnp.where(tile == column, 1.0, 0.0).astype(BF16)
    save(spread_by, spread_out)
    save(fold_by, fold_out)

    few_step(2)
    pass_on(2, segments_all)
    few_step(3)
    ring.step(0, 2)
    few_step(4)
    exchanged(2, segments_all, own_segments)
    numbers = pltpu.make_async_copy(segments_all, seg, seg_sems.at[0])
    numbers.start()
    for way in range(2):
        few_come(way, half - 1) if half < 2 else None
        few_come(way, half)
    own[0].wait()
    numbers.wait()

    numbers = jnp.concatenate([seg[k] for k in range(COPIES)], axis=0).astype(F32)
    lane = lax.broadcasted_iota(jnp.int32, (total, LANES), 1)
    time = lax.broadcasted_iota(jnp.int32, (total, LANES), 0) // GROUP
    picked = jnp.where(lane == time, jnp.concatenate([numbers] * length, axis=0), 0.0).astype(BF16)
    numbers = jnp.dot(picked, jnp.ones((LANES, LANES), BF16), preferred_element_type=F32)
    for shift in range(1, 4):
        earlier = jnp.concatenate(
            [jnp.full((shift * GROUP, LANES), -1.0, F32), numbers[: -shift * GROUP]], axis=0
        )
        masks[shift - 1] = jnp.where(earlier == numbers, 1.0, 0.0)
    save(masks, masks_out)
    save(few_all, few_out)
    first_small = 2 * rank + 2 * nstate
    small[...] = few_all[first_small : first_small + small.shape[0], :].astype(F32)
    taps, bias_row, skip_row, gain_row = 0, 5, 6 + nstate, 7 + nstate
    for n in range(nstate):
        rate[n] = jnp.broadcast_to(-LOG2E * jnp.exp(small[6 + n : 7 + n, :]), (GROUP, width))
    save(rate, rate_out)

    def fetch(source, t, slot):
        return pltpu.make_async_copy(
            source.at[:, pl.ds(pl.multiple_of(t * BLOCK, BLOCK), BLOCK), :], stage.at[slot], stage_sems.at[slot]
        )

    def weave(slot, scaled):
        for s in range(GROUP):
            value = stage[slot, s].astype(F32)
            if scaled:
                square = jnp.mean(value * value, axis=-1, keepdims=True)
                value = value * lax.rsqrt(square + EPS)
            for k in range(held.shape[0]):
                tile = value[:, k * LANES : (k + 1) * LANES]
                if scaled:
                    at = gain_row + k % 2
                    tile = tile * small[at : at + 1, (k // 2) * LANES : (k // 2 + 1) * LANES]
                held[k, pl.ds(s, BLOCK, stride=GROUP), :] = tile

    block_rows = BLOCK * GROUP
    blocks = total // block_rows

    def block_of(t):
        return pl.ds(pl.multiple_of(t * block_rows, block_rows), block_rows)

    pass_on(0, tokens_all)
    own_grads = exchange(1, out_grad, grads_all)
    ring.step(0, 3)
    exchanged(0, tokens_all, own_tokens)
    fetch(tokens_all, 0, 0).start()

    @pl.loop(0, blocks)
    def _(t):
        slot = lax.rem(t, 2)

        @pl.when(t + 1 < blocks)
        def _():
            fetch(tokens_all, t + 1, 1 - slot).start()

        @pl.when(t == blocks - 2)
        def _():
            ring.step(0, 4)
            ring.step(1, 1)

        fetch(tokens_all, t, slot).wait()
        weave(slot, True)
        for k in range(held.shape[0]):
            normed[block_of(t), k * LANES : (k + 1) * LANES] = held[k].astype(BF16)

    save(normed, normed_out)
    for copy in own_shards:
        copy.wait()
    ring.finish(0)
    save(w_in, w_in_out)

    def cotangent_out_of(t, slot):
        return pltpu.make_async_copy(cotangent.at[slot], cotangent_out.at[block_of(t), :], out_sems.at[slot])

    def weave_grads(first, count):
        fetch(grads_all, first, first % 2).start()

        @pl.loop(first, first + count)
        def _(t):
            slot = lax.rem(t, 2)

            @pl.when(t + 1 < first + count)
            def _():
                fetch(grads_all, t + 1, 1 - slot).start()

            @pl.when(t >= 2)
            def _():
                cotangent_out_of(t - 2, slot).wait()

            fetch(grads_all, t, slot).wait()
            weave(slot, False)
            for k in range(held.shape[0]):
                cotangent[slot, :, k * LANES : (k + 1) * LANES] = held[k].astype(BF16)
            cotangent_out_of(t, slot).start()

    inner[0:pad, :] = jnp.zeros((pad, width), F32)
    part[...] = jnp.zeros_like(part)

    @pl.loop(0, width // chunk)
    def _(c):
        cols = pl.ds(pl.multiple_of(c * chunk, chunk), chunk)
        inner[pad:, cols] = jnp.dot(normed[...], w_in[:, cols], preferred_element_type=F32)

        @pl.when(c == 1)
        def _():
            ring.step(2, 1)

        tap = [small[taps + i : taps + i + 1, cols] for i in range(5)]

        @pl.loop(0, total // rows)
        def _(i):
            start = pl.multiple_of(i * rows, rows)
            value = tap[4] + tap[3] * inner[pl.ds(pad + start, rows), cols]
            for shift in range(1, 4):
                mask = tiled(masks[shift - 1, pl.ds(start, rows), :], chunk)
                before = inner[pl.ds(pad - shift * GROUP + start, rows), cols]
                value = value + tap[3 - shift] * (before * mask)
            here = value * sigmoid(value)
            act[pl.ds(start, rows), cols] = here
            low[pl.ds(start, rows), cols] = here.astype(BF16)

        for j in range(2):
            part[j] += lax.dot_general(
                low[:, cols], few_all[j * LANES : (j + 1) * LANES, cols], (((1,), (1,)), ((), ())),
                preferred_element_type=F32,
            )

    save(inner.at[pl.ds(pad, total), :], inner_out)
    save(act, act_out)
    save(low, low_out)

    near = (near_send, near_recv)
    for j in range(2):
        for s in range(GROUP):
            nat[j, s * length : (s + 1) * length, :] = part[j, pl.ds(s, length, stride=GROUP), :]
    sends = []

    def start(source, target, index, peer):
        copy = remote(source, target, near, index, peer)
        copy.start()
        sends.append(copy)

    def come(target, index, peer):
        remote(target, target, near, index, peer).wait_recv()

    for i in range(2):
        start(nat.at[:, pl.ds((2 * i + 1) * side_rows, side_rows), :], got_near.at[i], i, peers.core)
    ring.step(1, 2)
    pass_on(1, grads_all)
    for i in range(2):
        come(got_near.at[i], i, peers.core)
    to_across[...] = nat[:, 2 * side_rows : 3 * side_rows, :] + got_near[1]
    start(to_across, got_across, 2, peers.across)
    exchanged(1, grads_all, own_grads)
    weave_grads(0, blocks // 2)
    ring.step(2, 2)
    come(got_across, 2, peers.across)
    mine = nat[:, :side_rows, :] + got_near[0] + got_across[...]
    shared[0, 0] = mine[0].astype(BF16)
    lane = lax.broadcasted_iota(jnp.int32, (side_rows, LANES), 1)
    rest, terms = jnp.where(lane < 2 * nstate, mine[1], 0.0), jnp.zeros((side_rows, LANES), F32)
    for i in range(3):
        term = rest.astype(BF16).astype(F32)
        rest = rest - term
        terms = terms + (pltpu.roll(term, 2 * nstate * i, 1) if i else term)
    shared[0, 1] = terms.astype(BF16)
    start(shared.at[0], shared.at[2], 3, peers.across)
    start(shared.at[0], shared.at[1], 4, peers.core)
    weave_grads(blocks // 2, blocks // 2)
    come(shared.at[2], 3, peers.across)
    start(shared.at[2], shared.at[3], 5, peers.core)
    come(shared.at[1], 4, peers.core)
    come(shared.at[3], 5, peers.core)
    for copy in sends:
        copy.wait_send()
    for k in range(COPIES):
        for b in range(batches):
            for j in range(2):
                part[j, pl.ds(k * batches + b, length, stride=GROUP), :] = shared[
                    k, j, b * length : (b + 1) * length, :
                ].astype(F32)
    step_low[...] = part[0].astype(BF16)
    coef[...] = part[1].astype(BF16)
    save(step_low, step_low_out)
    save(coef, coef_out)

    stride = few_all[rank + 2 * nstate : 2 * rank + 2 * nstate, :]
    side_bias = small[bias_row : bias_row + 1, :]
    carry[...] = jnp.zeros_like(carry)

    def keep_start(t, slot):
        return pltpu.make_async_copy(start_at.at[slot], start_out.at[t], start_sems.at[slot])

    @pl.loop(0, blocks)
    def _(t):
        for tick, which, number in ((0, 1, 3), (2, 2, 3), (4, 1, 4), (6, 2, 4)):

            @pl.when(t == tick)
            def _(which=which, number=number):
                ring.step(which, number)

        base = pl.multiple_of(t * block_rows, block_rows)
        these = block_of(t)
        wide[...] = jnp.dot(coef[these, :], spread_by[...], preferred_element_type=F32)
        pre[...] = jnp.dot(step_low[these, :], stride, preferred_element_type=F32)
        for i in range(BLOCK // 2):
            sub = slice(i * 2 * GROUP, (i + 1) * 2 * GROUP)
            step[pl.ds(base + i * 2 * GROUP, 2 * GROUP), :] = softplus(pre[sub, :] + side_bias)
        slot = lax.rem(t, 2)

        @pl.when(t >= 2)
        def _():
            keep_start(t - 2, slot).wait()

        start_at[slot] = carry[...]
        keep_start(t, slot).start()
        for c in range(width // chunk):
            cols = slice(c * chunk, (c + 1) * chunk)

            def advance(i, states):
                at = pl.ds(pl.multiple_of(base + i * GROUP, GROUP), GROUP)
                here = at_time(i)
                step_t, act_t = step[at, cols], act[at, cols]
                drive = jnp.where(tiled(masks[0, at, :], chunk) > 0.5, step_t, FAR)
                inflow = step_t * act_t
                out = small[skip_row : skip_row + 1, cols] * act_t
                now = []
                for n in range(nstate):
                    write = tiled(wide[here, n * LANES : (n + 1) * LANES], chunk)
                    read = tiled(wide[here, (nstate + n) * LANES : (nstate + n + 1) * LANES], chunk)
                    state = jnp.exp2(drive * rate[n, :, cols]) * states[n] + write * inflow
                    out = out + read * state
                    now.append(state)
                readout[at, cols] = out
                return tuple(now)

            states = lax.fori_loop(
                0, BLOCK, advance, tuple(carry[n, :, cols] for n in range(nstate)), unroll=4
            )
            for n in range(nstate):
                carry[n, :, cols] = states[n]

    save(step, step_out)
    save(readout, readout_out)

    ring.finish(1)
    save(gate_w, gate_w_out)

    def keep_gate(c, slot):
        cols = pl.ds(pl.multiple_of(c * chunk, chunk), chunk)
        return pltpu.make_async_copy(gate.at[slot], gate_out.at[:, cols], gate_sems.at[slot])

    @pl.loop(0, width // chunk)
    def _(c):
        cols = pl.ds(pl.multiple_of(c * chunk, chunk), chunk)
        slot = lax.rem(c, 2)

        @pl.when(c >= 2)
        def _():
            keep_gate(c - 2, slot).wait()

        gate[slot] = jnp.dot(normed[...], gate_w[:, cols], preferred_element_type=F32)
        keep_gate(c, slot).start()

        @pl.loop(0, total // rows)
        def _(i):
            at = pl.ds(pl.multiple_of(i * rows, rows), rows)
            here = gate[slot, at, :]
            value = readout[at, cols] * (here * sigmoid(here))
            gated[at, cols] = value.astype(BF16)
            for k in range(chunk // LANES):
                nat[k, at, :] = value[:, k * LANES : (k + 1) * LANES]

        for k in range(chunk // LANES):
            for s in range(GROUP):
                natural[s * length : (s + 1) * length, pl.ds(pl.multiple_of(c * chunk + k * LANES, LANES), LANES)] = nat[
                    k, pl.ds(s, length, stride=GROUP), :
                ].astype(BF16)

    save(gated, gated_out)
    save(natural, natural_out)
    own[1].wait()
    ring.finish(2)
    ring.sent_all()
    for moving in sent:
        moving.wait_send()
    for slot in range(2):
        keep_start(blocks - 2 + slot, slot).wait()
        keep_gate(width // chunk - 2 + slot, slot).wait()
        cotangent_out_of(blocks - 2 + slot, slot).wait()
    for copy in saved:
        copy.wait()


def forward(size, rank, nstate, entry, few, tokens, out_grad, segments, out_proj):
    batches, length, model = tokens.shape
    total = COPIES * batches * length
    slab, width = entry.shape[0], size * LANES
    blocks = length // BLOCK
    anywhere = pl.BlockSpec(memory_space=pl.ANY)
    half = size // 2
    dma = pltpu.SemaphoreType.DMA
    shape = jax.ShapeDtypeStruct
    full, low = shape((total, width), F32), shape((total, width), BF16)
    thin = shape((total, LANES), BF16)
    rows = shape((total, model), BF16)
    weights = shape((size * slab, width), BF16)
    few_all = shape((few.shape[0], width), BF16)
    masks = shape((3, total, LANES), F32)
    state = shape((nstate, GROUP, width), F32)
    spread_by = shape((LANES, 2 * nstate * LANES), BF16)
    fold_by = shape((2 * nstate * LANES, LANES), BF16)
    outs = dict(
        few=few_all,
        masks=masks,
        rate=state,
        spread_by=spread_by,
        fold_by=fold_by,
        normed=rows,
        cotangent=rows,
        tokens_all=shape((GROUP, length, model), BF16),
        grads_all=shape((GROUP, length, model), BF16),
        segments_all=shape((COPIES,) + segments.shape, segments.dtype),
        inner_in=weights,
        inner=full,
        act=full,
        act_low=low,
        step_low=thin,
        coef=thin,
        step=full,
        starts=shape((blocks,) + state.shape, F32),
        gate=full,
        readout=full,
        gated=low,
        gated_natural=low,
        gate_in=weights,
        out_w=shape((size * out_proj.shape[0] // COPIES, model), BF16),
    )
    quarter = total // COPIES
    scratch = [
        few_all,
        shape((few.shape[0] - 2 * rank - 2 * nstate, width), F32),
        masks,
        state,
        spread_by,
        fold_by,
        rows,
        shape((2, GROUP, BLOCK, model), BF16),
        shape((2, BLOCK * GROUP, model), BF16),
        shape((model // LANES, BLOCK * GROUP, LANES), F32),
        shape((COPIES,) + segments.shape, segments.dtype),
        shape((slab, width), BF16),
        shape((slab, width), BF16),
        weights,
        shape((total + 3 * GROUP, width), F32),
        full,
        low,
        shape((2, total, LANES), F32),
        shape((2, total, LANES), F32),
        shape((2, 2, quarter, LANES), F32),
        shape((2, quarter, LANES), F32),
        shape((2, quarter, LANES), F32),
        shape((COPIES, 2, quarter, LANES), BF16),
        thin,
        thin,
        shape((BLOCK * GROUP, 2 * nstate * LANES), F32),
        shape((BLOCK * GROUP, width), F32),
        full,
        full,
        state,
        shape((2,) + state.shape, F32),
        shape((2, total, 256), F32),
        low,
        low,
        weights,
    ]
    sems = [(20,), (2,), (2,), (7,), (2 * size,), (2,), (2,), (1,)]
    sems += [(3, 2, half, 2)] * 2 + [(2, half)] * 2 + [(3, 3)] * 2 + [(6,)] * 2
    results = pl.pallas_call(
        functools.partial(forward_kernel, size, rank, nstate),
        in_specs=[anywhere] * 6,
        out_specs=[anywhere] * len(outs),
        out_shape=list(outs.values()),
        scratch_shapes=[pltpu.VMEM(x.shape, x.dtype) for x in scratch] + [dma(n) for n in sems],
        compiler_params=pltpu.CompilerParams(
            collective_id=4, has_side_effects=True, vmem_limit_bytes=62 * 1024 * 1024
        ),
        cost_estimate=cost(8 * total * width * model, 100 * total * width),
        name="forward",
    )(entry, few, tokens, out_grad, segments, out_proj)
    return dict(zip(outs, results))


class Guests:
    def __init__(self, peers, parts, totals, held, sems):
        self.peers = peers
        self.parts, self.totals, self.held, self.sems = parts, totals, held, sems

    def rows(self, which, c):
        half = self.parts[which].shape[1] // 2
        return pl.ds(c * half, half)

    def copy(self, which, way, step, c, source=None):
        target = self.held[which].at[way, step - 1, self.rows(which, c), :]
        index = (which, way, step - 1, c)
        source = target if source is None else source
        return remote(source, target, self.sems, index, self.peers.ring[way])

    def chunks(self, way, step):
        return (way,) if step == 1 else (0, 1)

    def own(self, which, way, step, c):
        away = self.peers.half + 1 - step
        block = self.peers.at(away if way == 0 else -away)
        return self.parts[which].at[block, self.rows(which, c), :]

    def source(self, which, way, step, c):
        own = self.own(which, way, step, c)
        if step == 1 or c not in self.chunks(way, step - 1):
            return own
        self.copy(which, way, step - 1, c).wait_recv()
        there = self.held[which].at[way, step - 2, self.rows(which, c), :]
        there[...] = (own[...].astype(F32) + there[...].astype(F32)).astype(BF16)
        return there

    def step(self, which, step):
        for c in range(2):
            for way in range(2):
                if c in self.chunks(way, step):
                    self.copy(which, way, step, c, self.source(which, way, step, c)).start()

    def finish(self):
        last = self.peers.half
        for which in range(2):
            for c in range(2):
                total = self.own(which, 0, last + 1, c)[...].astype(F32)
                for way in range(2):
                    self.copy(which, way, last, c).wait_recv()
                    there = self.held[which].at[way, last - 1, self.rows(which, c), :]
                    total = total + there[...].astype(F32)
                self.totals[which][self.rows(which, c), :] = total.astype(BF16)
        for which in range(2):
            for step in range(1, last + 1):
                for way in range(2):
                    for c in self.chunks(way, step):
                        self.copy(which, way, step, c).wait_send()


def scan_back_kernel(
    nstate, chunk, step_ref, act_ref, grad_ref, coef_ref, spread_ref, fold_ref, keep_ref, rate_ref,
    row_ref, start_ref, *refs,
):
    wide, states_all, decays, parts, sizes = refs[-5:]
    width = step_ref.shape[1]
    step_now = pl.program_id(0)
    pre_grad_ref, direct_ref, coef_grad_ref, carry_ref, sums_ref = refs[-10:-5]

    @pl.when(step_now == 0)
    def _():
        carry_ref[...] = jnp.zeros_like(carry_ref)
        sums_ref[...] = jnp.zeros_like(sums_ref)

    wide[...] = jnp.dot(coef_ref[...], spread_ref[...], preferred_element_type=F32)

    def fold(value):
        total = value[:, :LANES]
        for k in range(1, chunk // LANES):
            total = total + value[:, k * LANES : (k + 1) * LANES]
        return total

    for c in range(width // chunk):
        cols = slice(c * chunk, (c + 1) * chunk)

        def advance(t, states):
            at = at_time(t)
            step = step_ref[at, cols]
            drive = jnp.where(tiled(keep_ref[at, :], chunk) > 0.5, step, FAR)
            inflow = step * act_ref[at, cols]
            now = []
            for n in range(nstate):
                write = tiled(wide[at, n * LANES : (n + 1) * LANES], chunk)
                decay = jnp.exp2(drive * rate_ref[n, :, cols])
                decays[t, n] = decay
                states_all[t, n] = states[n]
                now.append(decay * states[n] + write * inflow)
            return tuple(now)

        start = tuple(start_ref[0, n, :, cols] for n in range(nstate))
        states = lax.fori_loop(0, BLOCK, advance, start, unroll=2)
        for n in range(nstate):
            states_all[BLOCK, n] = states[n]

        def retreat(i, carry):
            t = BLOCK - 1 - i
            at = at_time(t)
            step, act, grad = step_ref[at, cols], act_ref[at, cols], grad_ref[at, cols]
            inflow = step * act
            size = jnp.zeros_like(step)
            direct = jnp.zeros_like(step)
            now = []
            for n in range(nstate):
                tile_w = slice(n * LANES, (n + 1) * LANES)
                tile_r = slice((nstate + n) * LANES, (nstate + n + 1) * LANES)
                state_grad = tiled(wide[at, tile_r], chunk) * grad + carry[n]
                passed = decays[t, n] * state_grad
                through = passed * states_all[t, n]
                size = size + rate_ref[n, :, cols] * through
                direct = direct + state_grad * tiled(wide[at, tile_w], chunk)
                sums_ref[n, :, cols] += step * through
                write_part = fold(state_grad * inflow)
                read_part = fold(grad * states_all[t + 1, n])
                if c == 0:
                    parts[at, tile_w] = write_part
                    parts[at, tile_r] = read_part
                else:
                    parts[at, tile_w] += write_part
                    parts[at, tile_r] += read_part
                now.append(passed)
            sizes[at, cols] = LN2 * size + act * direct
            direct_ref[at, cols] = step * direct + row_ref[1:2, cols] * grad
            sums_ref[nstate, :, cols] += grad * act
            return tuple(now)

        start = tuple(carry_ref[n, :, cols] for n in range(nstate))
        carry = lax.fori_loop(0, BLOCK, retreat, start, unroll=2)
        for n in range(nstate):
            carry_ref[n, :, cols] = carry[n]

    step = step_ref[...]
    series = step * (1.0 - step * (0.5 - step * (1.0 / 6.0)))
    pre_grad = sizes[...] * jnp.where(step < 0.01, series, 1.0 - jnp.exp(-step))
    pre_grad_ref[...] = pre_grad.astype(BF16)
    total = pre_grad[:GROUP]
    for t in range(1, BLOCK):
        total = total + pre_grad[t * GROUP : (t + 1) * GROUP]
    sums_ref[nstate + 1] += total
    high = parts[...].astype(BF16)
    low = (parts[...] - high.astype(F32)).astype(BF16)
    coef_grad_ref[...] = jnp.dot(high, fold_ref[...], preferred_element_type=F32) + jnp.dot(
        low, fold_ref[...], preferred_element_type=F32
    )


def scan_backward(
    step, act, grad, coef, spread_by, fold_by, keep, rate, rows, starts
):
    total, width = step.shape
    nstate = rate.shape[0]
    size = BLOCK * GROUP
    chunk = 256
    count = total // size
    tile = pl.BlockSpec((size, width), lambda t: (count - 1 - t, 0))
    thin = pl.BlockSpec((size, LANES), lambda t: (count - 1 - t, 0))
    state = pl.BlockSpec((nstate, GROUP, width), lambda t: (0, 0, 0))
    tally = pl.BlockSpec((nstate + 2, GROUP, width), lambda t: (0, 0, 0))
    work = count * size * width * nstate
    return pl.pallas_call(
        functools.partial(scan_back_kernel, nstate, chunk),
        grid=(count,),
        in_specs=[
            tile,
            tile,
            tile,
            thin,
            pl.BlockSpec(spread_by.shape, lambda t: (0, 0)),
            pl.BlockSpec(fold_by.shape, lambda t: (0, 0)),
            thin,
            state,
            pl.BlockSpec((8, width), lambda t: (0, 0)),
            pl.BlockSpec((1, nstate, GROUP, width), lambda t: (count - 1 - t, 0, 0, 0)),
        ],
        out_specs=[tile, tile, thin, state, tally],
        out_shape=[
            jax.ShapeDtypeStruct((total, width), BF16),
            jax.ShapeDtypeStruct((total, width), F32),
            jax.ShapeDtypeStruct((total, LANES), F32),
            jax.ShapeDtypeStruct((nstate, GROUP, width), F32),
            jax.ShapeDtypeStruct((nstate + 2, GROUP, width), F32),
        ],
        scratch_shapes=[
            pltpu.VMEM((size, 2 * nstate * LANES), F32),
            pltpu.VMEM((BLOCK + 1, nstate, GROUP, chunk), F32),
            pltpu.VMEM((BLOCK, nstate, GROUP, chunk), F32),
            pltpu.VMEM((size, 2 * nstate * LANES), F32),
            pltpu.VMEM((size, width), F32),
        ],
        compiler_params=params(),
        cost_estimate=cost(40 * work, 24 * count * size * width),
        name="scan_backward",
    )(step, act, grad, coef, spread_by, fold_by, keep, rate, rows, starts)


def backward_kernel(
    size, nstate, rank,
    gated_in, cotangent_in, w_out, readout_in, gate_in, normed_in, step_in, act_in, coef_in, starts_in, masks_in, rate_in,
    spread_in, fold_in, few_in,
    natural_out, pre_low_out, direct_out, coef_grad_out, sums_out, out_total, gate_total,
    gated, cotangent, out_w, normed, out_wgrad, gate_wgrad, out_held, gate_held, gate_grad, natural, grad, nat,
    step_at, act_at, start_at, wide, states_all, decays, parts, sizes, sums, carry, coef, spread_by, fold_by, rate, keep, few,
    coef_grad,
    load_sems, tile_sems, block_sems, save_sems, block_saves, ring_send, ring_recv,
):
    peers = Peers(size)
    total, width = gated.shape
    model = normed.shape[1]
    length = total // GROUP
    chunk, rows = 256, 64
    block_rows = BLOCK * GROUP
    blocks = total // block_rows
    loads, saved = {}, []

    def load(name, source, target):
        loads[name] = pltpu.make_async_copy(source, target, load_sems.at[len(loads)])
        loads[name].start()

    def save(source, target):
        saved.append(pltpu.make_async_copy(source, target, save_sems.at[len(saved)]))
        saved[-1].start()

    first_small = 2 * rank + 2 * nstate
    load("gated", gated_in, gated)
    load("cotangent", cotangent_in, cotangent)
    load("out_w", w_out, out_w)
    load("normed", normed_in, normed)
    load("coef", coef_in, coef)
    load("spread", spread_in, spread_by)
    load("fold", fold_in, fold_by)
    load("rate", rate_in, rate)
    load("keep", masks_in.at[0], keep)
    load("few", few_in.at[pl.ds(first_small, few.shape[0]), :], few)

    def tile_copies(c, slot):
        cols = pl.ds(pl.multiple_of(c * chunk, chunk), chunk)
        there = pl.ds(pl.multiple_of(slot * total, total), total)
        return [
            pltpu.make_async_copy(gate_in.at[:, cols], decays.at[there, :], tile_sems.at[0, slot]),
            pltpu.make_async_copy(readout_in.at[:, cols], states_all.at[there, :], tile_sems.at[1, slot]),
        ]

    for copy in tile_copies(0, 0):
        copy.start()
    peers.meet()
    ring = Guests(
        peers, (out_wgrad, gate_wgrad), None, (out_held, gate_held), (ring_send, ring_recv)
    )
    loads["gated"].wait()
    loads["cotangent"].wait()
    tn = (((0,), (0,)), ((), ()))
    nt = (((1,), (1,)), ((), ()))

    @pl.loop(0, model // chunk)
    def _(c):
        cols = pl.ds(pl.multiple_of(c * chunk, chunk), chunk)
        value = lax.dot_general(gated[...], cotangent[:, cols], tn, preferred_element_type=F32)
        out_wgrad[:, :, cols] = value.astype(BF16).reshape(size, -1, chunk)

    ring.step(0, 1)
    loads["out_w"].wait()

    @pl.loop(0, width // chunk)
    def _(c):
        cols = pl.ds(pl.multiple_of(c * chunk, chunk), chunk)
        slot = lax.rem(c, 2)

        @pl.when(c + 1 < width // chunk)
        def _():
            for copy in tile_copies(c + 1, 1 - slot):
                copy.start()

        @pl.when(c == 2)
        def _():
            ring.step(0, 2)

        grad[:, cols] = lax.dot_general(cotangent[...], out_w[cols, :], nt, preferred_element_type=F32)
        for copy in tile_copies(c, slot):
            copy.wait()

        @pl.loop(0, total // rows)
        def _(i):
            start = pl.multiple_of(i * rows, rows)
            at = pl.ds(start, rows)
            there = pl.ds(pl.multiple_of(slot * total + start, rows), rows)
            gate, readout, value = decays[there, :], states_all[there, :], grad[at, cols]
            sig = sigmoid(gate)
            grad[at, cols] = value * (gate * sig)
            value = value * readout * (sig * (1.0 + gate * (1.0 - sig)))
            gate_grad[at, cols] = value.astype(BF16)
            for k in range(chunk // LANES):
                nat[k, at, :] = value[:, k * LANES : (k + 1) * LANES]

        for k in range(chunk // LANES):
            lanes = pl.ds(pl.multiple_of(c * chunk + k * LANES, LANES), LANES)
            for s in range(GROUP):
                natural[s * length : (s + 1) * length, lanes] = nat[
                    k, pl.ds(s, length, stride=GROUP), :
                ].astype(BF16)

    save(natural, natural_out)

    def block_copies(t, slot):
        these = pl.ds(pl.multiple_of(t * block_rows, block_rows), block_rows)
        return [
            pltpu.make_async_copy(step_in.at[these, :], step_at.at[slot], block_sems.at[0, slot]),
            pltpu.make_async_copy(act_in.at[these, :], act_at.at[slot], block_sems.at[1, slot]),
            pltpu.make_async_copy(starts_in.at[t], start_at.at[slot], block_sems.at[2, slot]),
        ]

    for copy in block_copies(blocks - 1, (blocks - 1) % 2):
        copy.start()
    loads["normed"].wait()

    @pl.loop(0, width // chunk)
    def _(c):
        cols = pl.ds(pl.multiple_of(c * chunk, chunk), chunk)
        value = lax.dot_general(normed[...], gate_grad[:, cols], tn, preferred_element_type=F32)
        gate_wgrad[:, :, cols] = value.astype(BF16).reshape(size, -1, chunk)

    ring.step(1, 1)
    for name in ("coef", "spread", "fold", "rate", "keep", "few"):
        loads[name].wait()
    pre_low = gated
    skip_at = 6 + nstate
    skip_row = few[...].astype(F32)[skip_at : skip_at + 1]
    carry[...] = jnp.zeros_like(carry)
    sums[...] = jnp.zeros_like(sums)

    def fold(value):
        out = value[:, :LANES]
        for k in range(1, chunk // LANES):
            out = out + value[:, k * LANES : (k + 1) * LANES]
        return out

    def block_keeps(t):
        these = pl.ds(pl.multiple_of(t * block_rows, block_rows), block_rows)
        return [
            pltpu.make_async_copy(pre_low.at[these, :], pre_low_out.at[these, :], block_saves.at[0, t]),
            pltpu.make_async_copy(grad.at[these, :], direct_out.at[these, :], block_saves.at[1, t]),
        ]

    @pl.loop(0, blocks)
    def _(turn):
        t = blocks - 1 - turn
        slot = lax.rem(t, 2)
        for tick, which, number in ((0, 0, 3), (1, 1, 2), (3, 0, 4), (4, 1, 3), (6, 1, 4)):

            @pl.when(turn == tick)
            def _(which=which, number=number):
                ring.step(which, number)

        @pl.when(t > 0)
        def _():
            for copy in block_copies(t - 1, 1 - slot):
                copy.start()

        base = pl.multiple_of(t * block_rows, block_rows)
        these = pl.ds(base, block_rows)
        wide[...] = jnp.dot(coef[these, :], spread_by[...], preferred_element_type=F32)
        for copy in block_copies(t, slot):
            copy.wait()

        for c in range(width // chunk):
            cols = slice(c * chunk, (c + 1) * chunk)

            def entry(i, n):
                return pl.ds(pl.multiple_of((i * nstate + n) * GROUP, GROUP), GROUP)

            def advance(i, states):
                here = at_time(i)
                at = pl.ds(pl.multiple_of(base + i * GROUP, GROUP), GROUP)
                step = step_at[slot, here, cols]
                drive = jnp.where(tiled(keep[at, :], chunk) > 0.5, step, FAR)
                inflow = step * act_at[slot, here, cols]
                now = []
                for n in range(nstate):
                    write = tiled(wide[here, n * LANES : (n + 1) * LANES], chunk)
                    decay = jnp.exp2(drive * rate[n, :, cols])
                    decays[entry(i, n), :] = decay
                    states_all[entry(i, n), :] = states[n]
                    now.append(decay * states[n] + write * inflow)
                return tuple(now)

            start = tuple(start_at[slot, n, :, cols] for n in range(nstate))
            states = lax.fori_loop(0, BLOCK, advance, start, unroll=2)
            for n in range(nstate):
                states_all[entry(BLOCK, n), :] = states[n]

            def retreat(i, carried):
                i = BLOCK - 1 - i
                here = at_time(i)
                at = pl.ds(pl.multiple_of(base + i * GROUP, GROUP), GROUP)
                step, act, flow = step_at[slot, here, cols], act_at[slot, here, cols], grad[at, cols]
                inflow = step * act
                size_grad, direct = jnp.zeros_like(step), jnp.zeros_like(step)
                now = []
                for n in range(nstate):
                    tile_w = slice(n * LANES, (n + 1) * LANES)
                    tile_r = slice((nstate + n) * LANES, (nstate + n + 1) * LANES)
                    state_grad = tiled(wide[here, tile_r], chunk) * flow + carried[n]
                    passed = decays[entry(i, n), :] * state_grad
                    through = passed * states_all[entry(i, n), :]
                    size_grad = size_grad + rate[n, :, cols] * through
                    direct = direct + state_grad * tiled(wide[here, tile_w], chunk)
                    sums[n, :, cols] += step * through
                    write_part = fold(state_grad * inflow)
                    read_part = fold(flow * states_all[entry(i + 1, n), :])
                    if c == 0:
                        parts[here, tile_w] = write_part
                        parts[here, tile_r] = read_part
                    else:
                        parts[here, tile_w] += write_part
                        parts[here, tile_r] += read_part
                    now.append(passed)
                sizes[here, cols] = LN2 * size_grad + act * direct
                grad[at, cols] = step * direct + skip_row[:, cols] * flow
                sums[nstate, :, cols] += flow * act
                return tuple(now)

            start = tuple(carry[n, :, cols] for n in range(nstate))
            carried = lax.fori_loop(0, BLOCK, retreat, start, unroll=2)
            for n in range(nstate):
                carry[n, :, cols] = carried[n]

        step = step_at[slot]
        series = step * (1.0 - step * (0.5 - step * (1.0 / 6.0)))
        pre_grad = sizes[...] * jnp.where(step < 0.01, series, 1.0 - jnp.exp(-step))
        pre_low[these, :] = pre_grad.astype(BF16)
        tally = pre_grad[:GROUP]
        for i in range(1, BLOCK):
            tally = tally + pre_grad[i * GROUP : (i + 1) * GROUP]
        sums[nstate + 1] += tally
        high = parts[...].astype(BF16)
        low = (parts[...] - high.astype(F32)).astype(BF16)
        coef_grad[these, :] = jnp.dot(high, fold_by[...], preferred_element_type=F32) + jnp.dot(
            low, fold_by[...], preferred_element_type=F32
        )
        for copy in block_keeps(t):
            copy.start()

    save(coef_grad, coef_grad_out)
    save(sums, sums_out)
    ring.totals = (out_total, gate_total)
    ring.finish()
    for t in range(blocks):
        for copy in block_keeps(t):
            copy.wait()
    for copy in saved:
        copy.wait()


def backward(size, nstate, rank, arrays):
    gated, cotangent, w_out, readout, gate, normed, step, act, coef, starts, masks, rate, spread_by, fold_by, few = arrays
    total, width = gated.shape
    model = normed.shape[1]
    inside, anywhere = pl.BlockSpec(memory_space=pltpu.VMEM), pl.BlockSpec(memory_space=pl.ANY)
    shape, dma = jax.ShapeDtypeStruct, pltpu.SemaphoreType.DMA
    low, rows, full = shape((total, width), BF16), shape((total, model), BF16), shape((total, width), F32)
    out_unit, gate_unit = (width // size, model), (model // size, width)
    half = size // 2
    block = shape((2, BLOCK * GROUP, width), F32)
    state = shape((nstate, GROUP, width), F32)
    tally = shape((nstate + 2, GROUP, width), F32)
    wide = shape((BLOCK * GROUP, 2 * nstate * LANES), F32)
    thin = shape((total, LANES), F32)
    scratch = [
        low,
        rows,
        shape(w_out.shape, BF16),
        rows,
        shape((size,) + out_unit, BF16),
        shape((size,) + gate_unit, BF16),
        shape((2, half) + out_unit, BF16),
        shape((2, half) + gate_unit, BF16),
        low,
        low,
        full,
        shape((2, total, LANES), F32),
        block,
        block,
        shape((2,) + state.shape, F32),
        wide,
        shape(((BLOCK + 1) * nstate * GROUP, 256), F32),
        shape((BLOCK * nstate * GROUP, 256), F32),
        wide,
        shape((BLOCK * GROUP, width), F32),
        tally,
        state,
        shape(coef.shape, BF16),
        shape(spread_by.shape, BF16),
        shape(fold_by.shape, BF16),
        state,
        thin,
        shape((few.shape[0] - 2 * rank - 2 * nstate, width), BF16),
        thin,
    ]
    blocks = total // (BLOCK * GROUP)
    sems = [(10,), (2, 2), (3, 2), (3,), (2, blocks), (2, 2, half, 2), (2, 2, half, 2)]
    return pl.pallas_call(
        functools.partial(backward_kernel, size, nstate, rank),
        in_specs=[anywhere] * len(arrays),
        out_specs=[anywhere] * 5 + [inside] * 2,
        out_shape=[low, low, full, thin, tally, shape(out_unit, BF16), shape(gate_unit, BF16)],
        scratch_shapes=[pltpu.VMEM(x.shape, x.dtype) for x in scratch] + [dma(n) for n in sems],
        compiler_params=pltpu.CompilerParams(
            collective_id=3, has_side_effects=True, vmem_limit_bytes=62 * 1024 * 1024
        ),
        cost_estimate=cost(6 * total * width * model, 200 * total * width),
        name="backward",
    )(*arrays)


def finish_kernel(
    size, rank, nstate,
    pre_low_in, coef_in, direct_in, inner_in, act_low_in, step_low_in, masks_in, few_in, normed_in, w_inner, w_gate,
    gate_grad_in, gated_in, w_out, sums_in, out_total, gate_total,
    inner_pieces, gate_pieces, out_pieces, small_pieces, out_sum, norm_sum,
    pre_low, part, nat, got_near, to_across, got_across, shared, low_grad, act_low, step_low, masks, few, normed, gate_grad,
    gated, inner, direct, grad, wgrad, held, small, small_low, small_held, out_w, out_parts,
    out_pair, norm_pair, out_far, norm_far, w_tiles, total_at, sums,
    load_sems, tile_sems, w_sems, near_send, near_recv, pair_send, pair_recv, ring_send, ring_recv, few_send, few_recv,
    piece_send, piece_recv, own_sems,
):
    peers = Peers(size)
    half = peers.half
    total, width = pre_low.shape
    model = normed.shape[1]
    length = total // GROUP
    batches = GROUP // COPIES
    quarter = total // COPIES
    chunk, rows, pad = 256, 64, 3 * GROUP
    tiles = width // chunk
    slab = held.shape[2]
    sent, loads = [], {}

    def load(name, source, target):
        loads[name] = pltpu.make_async_copy(source, target, load_sems.at[len(loads)])
        loads[name].start()

    def send(*copy):
        moving = remote(*copy)
        moving.start()
        sent.append(moving)

    def tile_copies(c, slot):
        cols = slice(c * chunk, (c + 1) * chunk)
        return [
            pltpu.make_async_copy(inner_in.at[:, cols], inner.at[slot, pl.ds(pad, total), :], tile_sems.at[0, slot]),
            pltpu.make_async_copy(direct_in.at[:, cols], direct.at[slot], tile_sems.at[1, slot]),
        ]

    load("pre", pre_low_in, pre_low)
    load("few", few_in, few)
    load("coef", coef_in, part.at[1])
    load("step", step_low_in, step_low)
    load("gated", gated_in, gated)
    load("out_w", w_out, out_w)
    load("act", act_low_in, act_low)
    load("masks", masks_in, masks.at[:, pl.ds(0, total), :])
    load("normed", normed_in, normed)
    load("sums", sums_in, sums)
    load("gate", gate_grad_in, gate_grad)
    for copy in tile_copies(0, 0):
        copy.start()
    peers.meet()

    near = (near_send, near_recv)

    def come(target, index, peer):
        remote(target, target, near, index, peer).wait_recv()

    first_stride = rank + 2 * nstate
    loads["pre"].wait()
    loads["few"].wait()
    part[0] = lax.dot_general(
        pre_low[...], few[first_stride : first_stride + rank, :], (((1,), (1,)), ((), ())),
        preferred_element_type=F32,
    )
    loads["coef"].wait()
    for j in range(2):
        for s in range(GROUP):
            nat[j, s * length : (s + 1) * length, :] = part[j, pl.ds(s, length, stride=GROUP), :]
    for i in range(2):
        send(nat.at[:, pl.ds((2 * i + 1) * quarter, quarter), :], got_near.at[i], near, i, peers.core)
    near_sends = list(sent)
    loads["step"].wait()
    small[first_stride : first_stride + rank, :] = lax.dot_general(
        step_low[...], pre_low[...], (((0,), (0,)), ((), ())), preferred_element_type=F32
    )
    for i in range(2):
        come(got_near.at[i], i, peers.core)
    to_across[...] = nat[:, 2 * quarter : 3 * quarter, :] + got_near[1]
    send(to_across, got_across, near, 2, peers.across)
    loads["gated"].wait()
    loads["out_w"].wait()

    def out_tiles(first, count):
        @pl.loop(first, first + count)
        def _(c):
            cols = pl.ds(pl.multiple_of(c * chunk, chunk), chunk)
            out_parts[:, cols] = jnp.dot(gated[...], out_w[:, cols], preferred_element_type=F32).astype(BF16)

    out_tiles(0, model // chunk // 2)
    come(got_across, 2, peers.across)
    mine = nat[:, :quarter, :] + got_near[0] + got_across[...]
    for j in range(2):
        shared[0, j] = mine[j].astype(BF16)
    send(shared.at[0], shared.at[2], near, 3, peers.across)
    send(shared.at[0], shared.at[1], near, 4, peers.core)
    out_tiles(model // chunk // 2, model // chunk // 2)
    come(shared.at[2], 3, peers.across)
    send(shared.at[2], shared.at[3], near, 5, peers.core)
    come(shared.at[1], 4, peers.core)
    come(shared.at[3], 5, peers.core)
    for copy in near_sends:
        copy.wait_send()
    for k in range(COPIES):
        for b in range(batches):
            for j in range(2):
                part[j, pl.ds(k * batches + b, length, stride=GROUP), :] = shared[
                    k, j, b * length : (b + 1) * length, :
                ].astype(F32)
    for j in range(2):
        low_grad[j] = part[j].astype(BF16)

    pair_sems, piece_sems = (pair_send, pair_recv), (piece_send, piece_recv)
    keeps = []

    def of_copy(ref, k):
        return ref.at[pl.ds(k * quarter, quarter), :]

    def exchange(index, parts, pair):
        for i in range(2):
            send(of_copy(parts, 2 * i + 1), pair.at[i], pair_sems, 3 * index + i, peers.core)

    def exchange_far(index, parts, pair, far):
        for i in range(2):
            remote(pair.at[i], pair.at[i], pair_sems, 3 * index + i, peers.core).wait_recv()
        there = of_copy(parts, 2)
        there[...] = (there[...].astype(F32) + pair[1].astype(F32)).astype(BF16)
        send(there, far, pair_sems, 3 * index + 2, peers.across)

    def exchanged(index, parts, pair, far):
        remote(far, far, pair_sems, 3 * index + 2, peers.across).wait_recv()
        return of_copy(parts, 0)[...].astype(F32) + pair[0].astype(F32) + far[...].astype(F32)

    def give(index, own, pieces):
        keeps.append(pltpu.make_async_copy(own, pieces[0], own_sems.at[index]))
        keeps[-1].start()
        send(own, pieces[2], piece_sems, (index, 0), peers.across)
        send(own, pieces[1], piece_sems, (index, 1), peers.core)

    def pass_on(index, pieces):
        remote(pieces[2], pieces[2], piece_sems, (index, 0), peers.across).wait_recv()
        send(pieces[2], pieces[3], piece_sems, (index, 2), peers.core)

    def given(index, pieces):
        for k, which in ((1, 1), (3, 2)):
            remote(pieces[k], pieces[k], piece_sems, (index, which), peers.core).wait_recv()

    def every(ref, *at):
        return [ref.at[(k, *at)] for k in range(COPIES)]

    exchange(0, out_parts, out_pair)
    give(0, out_total, every(out_pieces))
    give(1, gate_total, every(gate_pieces))

    loads["act"].wait()
    for j, n in ((0, rank), (1, 2 * nstate)):
        weights = lax.dot_general(
            low_grad[j], act_low[...], (((0,), (0,)), ((), ())), preferred_element_type=F32
        )
        small[j * rank : j * rank + n, :] = weights[:n]

    inner_grad, natural = gated, pre_low
    loads["masks"].wait()
    loads["normed"].wait()
    masks[:, total:, :] = jnp.zeros((3, pad, LANES), F32)
    grad[total:, :] = jnp.zeros((pad, chunk), F32)
    for slot in range(2):
        inner[slot, :pad, :] = jnp.zeros((pad, chunk), F32)
    first_tap = first_stride + rank
    ring_sems, few_sems = (ring_send, ring_recv), (few_send, few_recv)

    def block_rows(member, part_of=None):
        start = pl.multiple_of(member * slab, slab)
        if part_of is None:
            return pl.ds(start, slab)
        return pl.ds(start + part_of * (slab // 2), slab // 2)

    def owner(way, step):
        away = half + 1 - step
        return peers.at(away if way == 0 else -away)

    def landing(way, step, c):
        there = held.at[way, step - 1, :, slice(c * chunk, (c + 1) * chunk)]
        return there.at[pl.ds(way * (slab // 2), slab // 2), :] if step == 1 else there

    def arrive(way, step, c):
        there = landing(way, step, c)
        remote(there, there, ring_sems, (way, step - 1, c), peers.ring[way]).wait_recv()

    def ring_step(step, c):
        cols = slice(c * chunk, (c + 1) * chunk)
        for way in range(2):
            member = owner(way, step)
            if step == 1:
                source = wgrad.at[block_rows(member, way), cols]
            else:
                arrive(way, step - 1, c)
                source = held.at[way, step - 2, :, cols]
                if step == 2:
                    here, other = (slice(w * (slab // 2), (w + 1) * (slab // 2)) for w in (way, 1 - way))
                    source[other, :] = wgrad[block_rows(member, 1 - way), cols]
                    source[here, :] = (
                        source[here, :].astype(F32) + wgrad[block_rows(member, way), cols].astype(F32)
                    ).astype(BF16)
                else:
                    source[...] = (
                        source[...].astype(F32) + wgrad[block_rows(member), cols].astype(F32)
                    ).astype(BF16)
            send(source, landing(way, step, c), ring_sems, (way, step - 1, c), peers.ring[way])

    def fold_rows(value):
        out = value[:GROUP]
        for i in range(1, rows // GROUP):
            out = out + value[i * GROUP : (i + 1) * GROUP]
        return out

    for c in range(tiles):
        cols, slot = slice(c * chunk, (c + 1) * chunk), c % 2
        if c + 1 < tiles:
            for copy in tile_copies(c + 1, 1 - slot):
                copy.start()
        for copy in tile_copies(c, slot):
            copy.wait()
        here, there = inner.at[slot], direct.at[slot]
        there[...] += jnp.dot(low_grad[0], few[:rank, cols], preferred_element_type=F32) + jnp.dot(
            low_grad[1], few[rank : rank + LANES, cols], preferred_element_type=F32
        )
        tap = [few[first_tap : first_tap + 16, cols].astype(F32)[i : i + 1] for i in range(5)]

        def back(i, tallies):
            start = pl.multiple_of(i * rows, rows)
            at = pl.ds(start, rows)
            now = here[pl.ds(pad + start, rows), :]
            earlier = [
                here[pl.ds(pad - shift * GROUP + start, rows), :] * tiled(masks[shift - 1, at, :], chunk)
                for shift in range(1, 4)
            ]
            value = tap[4] + tap[3] * now
            for shift in range(1, 4):
                value = value + tap[3 - shift] * earlier[shift - 1]
            sig = sigmoid(value)
            flow = there[at, :] * (sig * (1.0 + value * (1.0 - sig)))
            grad[at, :] = flow
            terms = [flow * e for e in earlier[::-1]] + [flow * now, flow]
            return tuple(tally + fold_rows(term) for tally, term in zip(tallies, terms))

        zero = jnp.zeros((GROUP, chunk), F32)
        tallies = lax.fori_loop(0, total // rows, back, (zero,) * 5)
        for i, tally in enumerate(tallies):
            small[first_tap + i : first_tap + i + 1, cols] = jnp.sum(tally, axis=0, keepdims=True)

        @pl.loop(0, total // rows)
        def _(i):
            start = pl.multiple_of(i * rows, rows)
            at = pl.ds(start, rows)
            value = tap[3] * grad[at, :]
            for shift in range(1, 4):
                after_it = pl.ds(start + shift * GROUP, rows)
                value = value + tap[3 - shift] * (
                    grad[after_it, :] * tiled(masks[shift - 1, after_it, :], chunk)
                )
            inner_grad[at, cols] = value.astype(BF16)
            for k in range(chunk // LANES):
                nat[k, at, :] = value[:, k * LANES : (k + 1) * LANES]

        for k in range(chunk // LANES):
            lanes = slice(c * chunk + k * LANES, c * chunk + (k + 1) * LANES)
            for s in range(GROUP):
                natural[s * length : (s + 1) * length, lanes] = nat[
                    k, pl.ds(s, length, stride=GROUP), :
                ].astype(BF16)
        wgrad[:, cols] = lax.dot_general(
            normed[...], inner_grad[:, cols], (((0,), (0,)), ((), ())), preferred_element_type=F32
        ).astype(BF16)
        ring_step(1, c)
        if c == 1:
            exchange_far(0, out_parts, out_pair, out_far)
        if c >= 2:
            ring_step(2, c - 2)

    loads["sums"].wait()
    at = first_tap + 5
    small[at : at + 1, :] = jnp.sum(sums[nstate + 1], axis=0, keepdims=True)
    decays = few[first_tap : first_tap + 32, :].astype(F32)
    for n in range(nstate):
        small[at + 1 + n : at + 2 + n, :] = -jnp.exp(decays[6 + n : 7 + n]) * jnp.sum(
            sums[n], axis=0, keepdims=True
        )
    at = at + 1 + nstate
    small[at : at + 1, :] = jnp.sum(sums[nstate], axis=0, keepdims=True)
    small[at + 1 :, :] = jnp.zeros((small.shape[0] - at - 1, width), F32)
    small_low[...] = small[...].astype(BF16)
    few_half = small.shape[0] // 2

    def few_columns(member):
        return pl.ds(pl.multiple_of(member * LANES, LANES), LANES)

    def few_landing(way, step):
        there = small_held.at[way, step - 1]
        return there.at[pl.ds(way * few_half, few_half), :] if step == 1 else there

    def few_arrive(way, step):
        there = few_landing(way, step)
        remote(there, there, few_sems, (way, step - 1), peers.ring[way]).wait_recv()

    def few_step(step):
        for way in range(2):
            columns = few_columns(owner(way, step))
            here, other = (slice(w * few_half, (w + 1) * few_half) for w in (way, 1 - way))
            if step == 1:
                source = small_low.at[pl.ds(way * few_half, few_half), columns]
            else:
                few_arrive(way, step - 1)
                source = small_held.at[way, step - 2]
                if step == 2:
                    source[other, :] = small_low[other, columns]
                    source[here, :] = (
                        source[here, :].astype(F32) + small_low[here, columns].astype(F32)
                    ).astype(BF16)
                else:
                    source[...] = (source[...].astype(F32) + small_low[:, columns].astype(F32)).astype(BF16)
            send(source, few_landing(way, step), few_sems, (way, step - 1), peers.ring[way])

    loads["gate"].wait()
    norm_parts = out_w

    def w_copies(n, slot):
        these = pl.ds(pl.multiple_of(n * chunk, chunk), chunk)
        return [
            pltpu.make_async_copy(w.at[these, :], w_tiles.at[slot, i], w_sems.at[i, slot])
            for i, w in enumerate((w_inner, w_gate))
        ]

    w_count = model // chunk

    def norm_tiles(first, count):
        @pl.loop(first, first + count)
        def _(n):
            slot = lax.rem(n, 2)

            @pl.when(n + 1 < w_count)
            def _():
                for copy in w_copies(n + 1, 1 - slot):
                    copy.start()

            for copy in w_copies(n, slot):
                copy.wait()
            nt = (((1,), (1,)), ((), ()))
            value = lax.dot_general(natural[...], w_tiles[slot, 0], nt, preferred_element_type=F32)
            value += lax.dot_general(gate_grad[...], w_tiles[slot, 1], nt, preferred_element_type=F32)
            norm_parts[:, pl.ds(pl.multiple_of(n * chunk, chunk), chunk)] = value.astype(BF16)

    few_step(1)
    for copy in w_copies(0, 0):
        copy.start()
    for i in range(2):
        norm_tiles(i, 1)
        ring_step(2, 2 + i)
    few_step(2)
    for i in range(4):
        norm_tiles(2 + i, 1)
        ring_step(3, i)
    few_step(3)
    norm_tiles(6, w_count - 6)
    own_rows = block_rows(peers.member)
    owns = [
        pltpu.make_async_copy(w_inner.at[own_rows, :], w_tiles.at[0, 0], w_sems.at[0, 0]),
        pltpu.make_async_copy(w_gate.at[own_rows, :], w_tiles.at[0, 1], w_sems.at[1, 0]),
        pltpu.make_async_copy(gate_total, w_tiles.at[1, 0], w_sems.at[0, 1]),
    ]
    for copy in owns:
        copy.start()
    exchange(1, norm_parts, norm_pair)
    ring_step(4, 0)
    ring_step(4, 1)
    exchange_far(1, norm_parts, norm_pair, norm_far)
    ring_step(4, 2)
    ring_step(4, 3)
    few_step(4)
    for index, pieces in ((0, out_pieces), (1, gate_pieces)):
        pass_on(index, every(pieces))
    out_sum[...] = exchanged(0, out_parts, out_pair, out_far)

    def cols_of(c):
        return slice(c * chunk, (c + 1) * chunk)

    def inner_views(c):
        return [inner_pieces.at[k, :, cols_of(c)] for k in range(COPIES)]

    own_block = block_rows(peers.member)
    for c in range(tiles):
        for way in range(2):
            arrive(way, half, c)
        value = wgrad[own_block, cols_of(c)].astype(F32)
        for way in range(2):
            value = value + held[way, half - 1, :, cols_of(c)].astype(F32)
        total_at[:, cols_of(c)] = value.astype(BF16)
        give(3 + c, total_at.at[:, cols_of(c)], inner_views(c))
    for way in range(2):
        few_arrive(way, half)
    value = small_low[:, few_columns(peers.member)].astype(F32)
    for way in range(2):
        value = value + small_held[way, half - 1].astype(F32)
    small_total = small_pieces.at[0]
    small_total[...] = value.astype(BF16)
    for copy in owns:
        copy.wait()
    value = total_at[...].astype(F32) * w_tiles[0, 0].astype(F32)
    value = value + w_tiles[1, 0].astype(F32) * w_tiles[0, 1].astype(F32)
    high = value.astype(BF16)
    low = (value - high.astype(F32)).astype(BF16)
    ones = jnp.ones((GROUP, width), BF16)
    nt = (((1,), (1,)), ((), ()))
    value = lax.dot_general(ones, high, nt, preferred_element_type=F32) + lax.dot_general(
        ones, low, nt, preferred_element_type=F32
    )
    gain_at = first_tap + 7 + nstate
    last = small_total[gain_at - gain_at % 16 :, :].astype(F32)
    line = lax.broadcasted_iota(jnp.int32, last.shape, 0) + (gain_at - gain_at % 16)
    for i in range(slab // LANES):
        last = jnp.where(line == gain_at + i, value[0:1, i * LANES : (i + 1) * LANES], last)
    small_total[gain_at - gain_at % 16 :, :] = last.astype(BF16)
    send(small_total, small_pieces.at[2], piece_sems, (2, 0), peers.across)
    send(small_total, small_pieces.at[1], piece_sems, (2, 1), peers.core)
    norm_sum[...] = exchanged(1, norm_parts, norm_pair, norm_far)
    for c in range(tiles):
        pass_on(3 + c, inner_views(c))
    pass_on(2, every(small_pieces))
    for index, pieces in ((0, every(out_pieces)), (1, every(gate_pieces)), (2, every(small_pieces))):
        given(index, pieces)
    for c in range(tiles):
        given(3 + c, inner_views(c))
    for copy in keeps:
        copy.wait()
    for moving in sent[len(near_sends) :]:
        moving.wait_send()


def finish(size, rank, nstate, arrays, small_rows):
    (pre_low, coef, direct, inner, act_low, step_low, masks, few, normed) = arrays[:9]
    total, width = pre_low.shape
    model = normed.shape[1]
    out_total, gate_total = arrays[-2:]
    slab = gate_total.shape[0]
    quarter, half = total // COPIES, size // 2
    inside, anywhere = pl.BlockSpec(memory_space=pltpu.VMEM), pl.BlockSpec(memory_space=pl.ANY)
    shape, dma = jax.ShapeDtypeStruct, pltpu.SemaphoreType.DMA
    low = shape((total, width), BF16)
    wide = shape((total, model), BF16)
    pair = shape((2, quarter, model), BF16)
    far = shape((quarter, model), BF16)
    sums = arrays[-3]
    padded = total + 3 * GROUP
    scratch = [
        low,
        shape((2, total, LANES), F32),
        shape((2, total, LANES), F32),
        shape((2, 2, quarter, LANES), F32),
        shape((2, quarter, LANES), F32),
        shape((2, quarter, LANES), F32),
        shape((COPIES, 2, quarter, LANES), BF16),
        shape((2, total, LANES), BF16),
        low,
        shape(step_low.shape, BF16),
        shape((3, padded, LANES), F32),
        shape(few.shape, BF16),
        wide,
        low,
        low,
        shape((2, padded, 256), F32),
        shape((2, total, 256), F32),
        shape((padded, 256), F32),
        shape((size * slab, width), BF16),
        shape((2, half, slab, width), BF16),
        shape((small_rows, width), F32),
        shape((small_rows, width), BF16),
        shape((2, half, small_rows, LANES), BF16),
        shape((max(width, total), model), BF16),
        wide,
        pair,
        pair,
        far,
        far,
        shape((2, 2, 256, width), BF16),
        shape((slab, width), BF16),
        shape(sums.shape, F32),
    ]
    tiles = width // 256
    sems = [(11,), (2, 2), (2, 2)] + [(6,)] * 2 + [(6,)] * 2 + [(2, half, tiles)] * 2 + [(2, half)] * 2
    sems += [(3 + tiles, 3)] * 2 + [(3 + tiles,)]
    return pl.pallas_call(
        functools.partial(finish_kernel, size, rank, nstate),
        in_specs=[anywhere] * len(arrays),
        out_specs=[anywhere] * 3 + [inside] * 3,
        out_shape=[
            shape((COPIES, slab, width), BF16),
            shape((COPIES, slab, width), BF16),
            shape((COPIES,) + out_total.shape, BF16),
            shape((COPIES, small_rows, LANES), BF16),
            shape((quarter, model), F32),
            shape((quarter, model), F32),
        ],
        scratch_shapes=[pltpu.VMEM(x.shape, x.dtype) for x in scratch] + [dma(n) for n in sems],
        compiler_params=pltpu.CompilerParams(
            collective_id=2, has_side_effects=True, vmem_limit_bytes=62 * 1024 * 1024
        ),
        cost_estimate=cost(10 * total * width * model, 100 * total * width),
        name="finish",
    )(*arrays)


def place_kernel(
    sizes, copy_ref, inner_ref, gate_ref, out_ref, small_ref, out_sum_ref, norm_ref, tokens_ref, grads_ref, few_ref,
    entry_ref, out_proj_ref, select_ref, stride_ref, taps_ref, decay_ref, rows_ref, block_out_ref, input_grad_ref,
):
    copy = copy_ref[0]
    width = inner_ref.shape[2]
    for k in range(COPIES):
        for side, ref in enumerate((inner_ref, gate_ref)):
            for f in range(width // LANES):
                start = (side * (width // LANES) + f) * COPIES * LANES + (copy ^ k) * LANES
                entry_ref[:, pl.ds(pl.multiple_of(start, LANES), LANES)] = ref[
                    k, :, f * LANES : (f + 1) * LANES
                ].astype(F32)
        out_proj_ref[copy ^ k] = out_ref[k].astype(F32)

    @pl.when(pl.program_id(0) == 0)
    def _():
        for k in range(COPIES):
            piece = small_ref[k].astype(F32)
            at = pl.ds(pl.multiple_of((copy ^ k) * LANES, LANES), LANES)
            stride_ref[at, :] = piece[sizes[0] : sizes[0] + sizes[1]].T
            start = 0
            for size, ref in zip(sizes, (select_ref, None, taps_ref, None, None, decay_ref)):
                if ref is not None:
                    ref[:, at] = piece[start : start + size]
                start += size
            first = start - start % 8
            low_row = sizes[0] + sizes[1]
            rows_ref[:, at] = jnp.concatenate(
                [piece[low_row : low_row + 8], piece[first : first + 8]], axis=0
            )

    tokens = tokens_ref[...].astype(F32)
    block_out_ref[...] = (tokens + out_sum_ref[...]).astype(BF16)
    gains = few_ref[...].astype(F32)
    start = sum(sizes) - (sizes[0] + sizes[1])
    gain = jnp.concatenate(
        [
            gains[start + i : start + i + 1, f * LANES : (f + 1) * LANES]
            for f in range(width // LANES)
            for i in range(tokens.shape[1] // width)
        ],
        axis=1,
    )
    scale = lax.rsqrt(jnp.mean(tokens * tokens, axis=-1, keepdims=True) + EPS)
    scaled = norm_ref[...] * gain
    lean = jnp.mean(scaled * tokens, axis=-1, keepdims=True)
    input_grad_ref[...] = (
        grads_ref[...].astype(F32) + scale * scaled - tokens * (scale * scale * scale) * lean
    ).astype(BF16)


def place(copy, sizes, inner, gate, out, small, out_sum, norm_sum, tokens, grads, few):
    steps = 4
    _, slab, width = inner.shape
    part, model = out.shape[1:]
    rows = tokens.shape[0]
    share = COPIES * LANES

    def cut_rows(total, columns):
        return pl.BlockSpec((total // steps, columns), lambda i, copy: (i, 0))

    def pieces(total, columns):
        return pl.BlockSpec((COPIES, total // steps, columns), lambda i, copy: (0, i, 0))

    def fixed(*shape):
        return pl.BlockSpec(shape, lambda i, copy: (0,) * len(shape))

    first = sizes[0] + sizes[1]
    last = few.shape[0] - first
    shape = jax.ShapeDtypeStruct
    narrow = [(sizes[0], share), (share, sizes[1]), (sizes[2], share), (sizes[5], share)]
    token_rows = cut_rows(rows, model)
    return pl.pallas_call(
        functools.partial(place_kernel, sizes),
        grid_spec=pltpu.PrefetchScalarGridSpec(
            num_scalar_prefetch=1,
            grid=(steps,),
            in_specs=[pieces(slab, width)] * 2
            + [pieces(part, model), fixed(*small.shape)]
            + [token_rows] * 4
            + [pl.BlockSpec((last, width), lambda i, copy: (first // last, 0))],
            out_specs=[cut_rows(slab, 2 * COPIES * width), pieces(part, model)]
            + [fixed(*n) for n in narrow]
            + [fixed(16, share)]
            + [token_rows] * 2,
        ),
        out_shape=[
            shape((slab, 2 * COPIES * width), F32),
            shape(out.shape, F32),
        ]
        + [shape(n, F32) for n in narrow]
        + [shape((16, share), F32)]
        + [shape(tokens.shape, BF16)] * 2,
        compiler_params=params(),
        cost_estimate=cost(40 * rows * model, 20 * slab * width),
        name="place",
    )(copy, inner, gate, out, small, out_sum, norm_sum, tokens, grads, few)


def on_device(
    tokens, segment_ids, out_grad, norm_gain, in_proj, conv_weight, conv_bias, x_proj,
    step_proj, step_bias, decay_log, skip_gain, out_proj, *, fsdp,
):
    ring = Ring(fsdp)
    copy = lax.axis_index("rep")
    batches, length, model = tokens.shape
    total = COPIES * batches * length
    slab = in_proj.shape[0]
    share = out_proj.shape[0]
    part = share // COPIES
    width = fsdp * part
    rank, nstate = step_proj.shape[1], decay_log.shape[1]
    taps_n = conv_weight.shape[1]
    gains_n = slab // part

    def mine(value):
        return lax.dynamic_slice_in_dim(value, copy * part, part, 0)

    copy_index = copy.astype(jnp.int32).reshape(1)
    aligned = part % LANES == 0
    if not aligned:
        entry = lax.dynamic_index_in_dim(
            in_proj.reshape(slab, 2, fsdp, COPIES, part), copy, 3, keepdims=False
        )
        inner_shard, gate_shard = (entry[:, i].reshape(slab, width) for i in range(2))
    few = jnp.concatenate(
        [
            mine(x_proj).T,
            mine(step_proj).T,
            mine(conv_weight).T,
            mine(conv_bias)[None],
            mine(step_bias)[None],
            mine(decay_log).T,
            mine(skip_gain)[None],
            norm_gain.reshape(gains_n, part),
        ],
        axis=0,
    )
    few = jnp.pad(few, ((0, -few.shape[0] % 16), (0, 0)))
    small_ring = ring.half == 4
    own = [tokens, out_grad, segment_ids[:, 0, :]]
    fused = small_ring and aligned
    if fused:
        out = forward(fsdp, rank, nstate, in_proj, few, *own, out_proj)
        few_all = out["few"].astype(F32)
    else:
        gathers = [Gather(ring, inner_shard), Gather(ring, few)]
        for gather in gathers:
            gather.rest()
        inner_in, few_all = (gather.whole for gather in gathers)
        few_all = jnp.moveaxis(few_all, 0, 1).reshape(-1, width).astype(F32)
        copies = [jnp.stack(rep_gather(value)) for value in own]
        inner_in = inner_in.reshape(model, width)
        values, cotangent, segments = (c.reshape((GROUP,) + c.shape[2:]) for c in copies)

    sizes = [rank + 2 * nstate, rank, taps_n, 1, 1, nstate, 1, gains_n]
    pieces, start = [], 0
    for size in sizes:
        pieces.append(few_all[start : start + size])
        start += size
    select, stride, taps, shift_bias, size_bias, decay, skip, gain = pieces
    select, stride = select.astype(BF16), stride.astype(BF16)
    gain = jnp.moveaxis(gain.reshape(gains_n, fsdp, part), 0, 1).reshape(model)

    def masks_of(segments):
        masks = []
        for shift in range(1, taps_n):
            earlier = jnp.pad(segments, ((0, 0), (shift, 0)), constant_values=-1)[:, :length]
            masks.append((earlier == segments).astype(F32).T.reshape(total, 1))
        return jnp.broadcast_to(jnp.stack(masks), (taps_n - 1, total, LANES))

    tap_rows = jnp.concatenate([taps, shift_bias, jnp.zeros((7 - taps_n, width), F32)])
    side_rows = jnp.concatenate([size_bias, skip, jnp.zeros((6, width), F32)])
    decay_rate = -jnp.exp(decay)

    if fused:
        (
            masks, rate, spread_by, fold_by, normed, cotangent, inner_in, inner, act, act_low, step_low, coef, step,
            starts, gate, readout, gated, gated_natural, gate_in, out_w,
        ) = (
            out[k]
            for k in (
                "masks", "rate", "spread_by", "fold_by", "normed", "cotangent", "inner_in", "inner", "act", "act_low",
                "step_low", "coef", "step", "starts", "gate", "readout", "gated", "gated_natural", "gate_in", "out_w",
            )
        )
    else:
        rate = jnp.broadcast_to((decay_rate * LOG2E)[:, None, :], (nstate, GROUP, width))
        masks, spread_by, fold_by = masks_of(segments), spreader(nstate), folder(nstate)
        normed, cotangent = interleave(values, gain), interleave(cotangent)
        gathers = [Gather(ring, gate_shard), Gather(ring, mine(out_proj))]
        for gather in gathers:
            gather.rest()
        gate_in = gathers[0].whole.reshape(model, width)
        out_w = gathers[1].whole.reshape(width, model)
        inner = dot(normed, inner_in, 1, 0)
        act, act_low = conv_forward(inner, masks, tap_rows)
        half_sums = sum_near(by_copy(to_sequence(dot(act_low, select, 1, 1))))
        projected = to_time(sum_far(half_sums).reshape(total, -1))
        step_low = projected[:, :rank].astype(BF16)
        coef = spread(projected[:, rank:], nstate)
        pre = dot(step_low, stride, 1, 0)
        readout, step, starts = scan_forward(pre, act, coef, spread_by, masks[0], rate, side_rows)
        gate = dot(normed, gate_in, 1, 0)
        gated, gated_natural = gate_forward(readout, gate)
    if fused:
        gate_grad_natural, pre_low, direct, coef_part, sums, *totals = backward(
            fsdp, nstate, rank,
            (
                gated, cotangent, out_w, readout, gate, normed, step, act, coef, starts, masks, rate, spread_by, fold_by,
                out["few"],
            ),
        )
    else:
        out_wgrad = dot(gated, cotangent, 0, 0).astype(BF16).reshape(fsdp, part, model)
        read_grad, gate_grad, gate_grad_natural = gate_backward(dot(cotangent, out_w, 1, 1), readout, gate)
        gate_wgrad = dot(normed, gate_grad, 0, 0).astype(BF16).reshape(fsdp, slab, width)
        pre_low, direct, coef_part, _, sums = scan_backward(
            step, act, read_grad, coef, spread_by, fold_by, masks[0], rate, side_rows, starts
        )
        scatters = [Scatter(ring, out_wgrad), Scatter(ring, gate_wgrad)]
        for scatter in scatters:
            scatter.rest()
        totals = [scatter.total.astype(BF16) for scatter in scatters]
    small_rows = few.shape[0]
    if fused:
        inner_pieces, gate_pieces, out_pieces, small_pieces, out_sum, normed_sum = finish(
            fsdp, rank, nstate,
            (
                pre_low, coef_part, direct, inner, act_low, step_low, masks, out["few"], normed, inner_in, gate_in,
                gate_grad_natural, gated_natural, out_w, sums, *totals,
            ),
            small_rows,
        )
        flat = (batches * length, model)
        entry_all, out_all, select_g, stride_g, taps_g, decay_g, rows_g, block_out, input_grad = place(
            copy_index, sizes[:-1], inner_pieces, gate_pieces, out_pieces, small_pieces, out_sum, normed_sum,
            tokens.reshape(flat), out_grad.reshape(flat), out["few"],
        )
        gain_at = sum(sizes[:-1])
        gain_sum = jnp.sum(small_pieces[:, gain_at : gain_at + gains_n].astype(F32), axis=0).reshape(slab)
        return (
            block_out.reshape(tokens.shape),
            input_grad.reshape(tokens.shape),
            gain_sum / norm_gain.astype(F32),
            entry_all,
            taps_g.T,
            rows_g[taps_n],
            select_g.T,
            stride_g,
            rows_g[taps_n + 1],
            decay_g.T,
            rows_g[8 + (gain_at - 1) % 8],
            out_all.reshape(share, model),
        )
    else:
        low_part = dot(pre_low, stride, 1, 1)
        proj_part = jnp.concatenate([low_part, coef_part[:, : 2 * nstate]], axis=1)
        half_sums = sum_near(by_copy(to_sequence(proj_part)))
        proj_time = to_time(sum_far(half_sums).reshape(total, -1).astype(BF16))
        act_grad = direct + dot(proj_time, select, 1, 0)
        inner_grad, inner_grad_natural, conv_sums = conv_backward(inner, act_grad, masks, tap_rows)
        inner_wgrad = dot(normed, inner_grad, 0, 0).astype(BF16).reshape(fsdp, slab, width)
        small = jnp.concatenate(
            [
                dot(proj_time, act_low, 0, 0),
                dot(step_low, pre_low, 0, 0),
                conv_sums[: taps_n + 1],
                jnp.sum(sums[nstate + 1 :], axis=1),
                decay_rate * jnp.sum(sums[:nstate], axis=1),
                jnp.sum(sums[nstate : nstate + 1], axis=1),
            ],
            axis=0,
        )
        small = jnp.pad(small, ((0, small_rows - small.shape[0]), (0, 0))).astype(BF16)
        small = jnp.moveaxis(small.reshape(-1, fsdp, part), 1, 0)
        grads = dot(inner_grad_natural, inner_in, 1, 1) + dot(gate_grad_natural, gate_in, 1, 1)
        sums_of = []
        for parts in (dot(gated_natural, out_w, 1, 0), grads):
            sums_of.append(rep_scatter_far(*rep_scatter_near(by_copy(parts.astype(BF16)))))
        out_sum, normed_sum = sums_of
        scatters = [Scatter(ring, inner_wgrad), Scatter(ring, small)]
        for scatter in scatters:
            scatter.rest()
        totals = [scatter.total.astype(BF16) for scatter in scatters] + totals
        inner_pieces, small_pieces, out_pieces, gate_pieces = (rep_gather(t) for t in totals)

    block_out = (tokens.astype(F32) + out_sum.reshape(tokens.shape)).astype(BF16)
    normed_grad = normed_sum.reshape(tokens.shape)
    own_values = tokens.astype(F32)
    own_scale = lax.rsqrt(jnp.mean(own_values * own_values, axis=-1, keepdims=True) + EPS)
    scaled = normed_grad * gain
    lean = jnp.mean(scaled * own_values, axis=-1, keepdims=True)
    input_grad = (
        out_grad.astype(F32) + own_scale * scaled - own_values * (own_scale**3) * lean
    ).astype(BF16)

    order = jnp.arange(COPIES) ^ copy
    out_all = jnp.stack(out_pieces)[order].reshape(share, model).astype(F32)
    halves = jnp.stack([jnp.stack(inner_pieces), jnp.stack(gate_pieces)])[:, order]
    halves = halves.reshape(2, COPIES, slab, fsdp, part).astype(F32)
    entry_all = jnp.transpose(halves, (2, 0, 3, 1, 4)).reshape(slab, -1)
    gain_sum = jnp.sum(entry_all * in_proj.astype(F32), axis=1)
    gain_grad = gain_sum / norm_gain.astype(F32)
    small_all = jnp.stack(small_pieces)[order].astype(F32)
    small_all = jnp.moveaxis(small_all, 0, 1).reshape(-1, share)
    out, start = [], 0
    for size in sizes[:-1]:
        out.append(small_all[start : start + size])
        start += size
    select_g, stride_g, taps_g, shift_g, size_g, decay_g, skip_g = out
    return (
        block_out,
        input_grad,
        gain_grad,
        entry_all,
        taps_g.T,
        shift_g[0],
        select_g.T,
        stride_g.T,
        size_g[0],
        decay_g.T,
        skip_g[0],
        out_all,
    )


def solution(mesh):
    tokens = P(None, ("fsdp", "rep"), None)
    rows, row = P("fsdp", None), P("fsdp")
    return jax.shard_map(
        functools.partial(on_device, fsdp=mesh.shape["fsdp"]),
        mesh=mesh,
        in_specs=(tokens, tokens, tokens, row, rows, rows, row, rows, rows, row, rows, row, rows),
        out_specs=(tokens, tokens, row, rows, rows, row, rows, rows, row, rows, row, rows),
        check_vma=False,
    )
```

profile of v0, /device:TPU:0, one launch (start us, length us, event | category | flops | bytes accessed | tf_op | source)
XLA Modules:
  0.0 387.7 jit_solution(12621358348204659988)
XLA Ops:
  0.6 0.0 copy-start
  0.7 0.8 dynamic-slice_bitcast_fusion.5
  1.5 0.7 dynamic-slice_bitcast_fusion.2
  2.1 0.8 dynamic-slice_bitcast_fusion.3
  2.9 0.7 dynamic-slice_bitcast_fusion.1
  3.6 0.8 constant_dynamic-slice_fusion
  4.4 0.1 copy.26
  4.5 0.0 copy-done
  4.5 0.9 concatenate.3
  5.4 0.6 pad.4.few
  6.1 150.3 %forward.1 = (bf16[320,1024]{1,0:T(8,128)(2,1)}, f32[3,1024,128]{2,1,0:T(8,128)}, f32[16,8,1024]{2,1,0:T(8,128)}, bf16[128,4096]{1,0:T(8,128)(2,1)}, bf16[4096,1...) custom-call(bf16[256,8192]{1,0:T(8,128)(2,1)} %entry.1, ...), custom_call_target="tpu_custom_call" | custom-call | flops 17179869184 | bytes 104857600 | tf_op jit(solution)/shard_map/forward/pallas_call | solution.py:1100
  156.4 102.9 %backward.1 = (bf16[1024,1024]{1,0:T(8,128)(2,1)}, bf16[1024,1024]{1,0:T(8,128)(2,1)}, f32[1024,1024]{1,0:T(8,128)}, f32[1024,128]{1,0:T(8,128)}, f32[18,8,1024]...) custom-call(bf16[1024,1024]{1,0:T(8,128)(2,1)} %get-tuple-element.55.gated_in, ...), custom_call_target="tpu_custom_call" | custom-call | flops 12884901888 | bytes 209715200 | tf_op jit(solution)/shard_map/backward/pallas_call | solution.py:1618
  259.3 0.0 copy-start.2
  259.3 115.0 %finish.1 = (bf16[4,256,1024]{2,1,0:T(8,128)(2,1)}, bf16[4,256,1024]{2,1,0:T(8,128)(2,1)}, bf16[4,128,2048]{2,1,0:T(8,128)(2,1)}, bf16[4,320,128]{2,1,0:T(8,128)...) custom-call(bf16[1024,1024]{1,0:T(8,128)(2,1)} %get-tuple-element.70.pre_low_in, f32[1024,128]{1,0:T(8,128)} %get-tuple-element.71.coef_in, ...), custom_call_target="tpu_custom_call" | custom-call | flops 21474836480 | bytes 104857600 | tf_op jit(solution)/shard_map/finish/pallas_call | solution.py:2123
  374.3 0.7 convert_reduce_fusion
  375.0 0.0 copy-done.2
  375.0 0.0 copy-start.1
  375.0 0.6 bitcast_divide_fusion
  375.6 10.5 %place.1 = (f32[256,8192]{1,0:T(8,128)}, f32[4,128,2048]{2,1,0:T(8,128)}, f32[160,512]{1,0:T(8,128)}, f32[512,128]{1,0:T(8,128)}, f32[4,512]{1,0:T(4,128)}, /*in...) custom-call(s32[1]{0:T(128)} %bitcast.copy_ref, ...), custom_call_target="tpu_custom_call" | custom-call | flops 20971520 | bytes 5242880 | tf_op jit(solution)/shard_map/place/pallas_call | solution.py:2217
  386.1 1.4 fusion
  387.5 0.0 copy-done.1
  (1 shorter events, 0.0 us)
Async XLA Ops:
  0.6 3.8 copy-start
  259.3 115.7 %copy-start.2 = (bf16[256]{0:T(256)(128)(2,1)S(1)}, bf16[256]{0:T(256)(128)(2,1)}, u32[]{:S(2)}) copy-start(bf16[256]{0:T(256)(128)(2,1)} %param.16) | copy-start | bytes 1540
  375.0 12.5 %copy-start.1 = (bf16[512,160]{0,1:T(8,128)(2,1)S(1)}, bf16[512,160]{0,1:T(8,128)(2,1)}, u32[]{:S(2)}) copy-start(bf16[512,160]{0,1:T(8,128)(2,1)} %param.20) | copy-start | bytes 491524
where the time goes:
time: 391 us; the launch traced here: 388 us
  Pallas kernels  379 us (97%)
  local copies, waits for them, and re-layouts  6.81 us (2%)
    pallas_call x1, Pallas kernels, forward(): pl.pallas_call(functools.partial(forward_kernel, size, rank, nstate), in_...  150 us
    pallas_call x1, Pallas kernels, finish(): pl.pallas_call(functools.partial(finish_kernel, size, rank, nstate), in_s...  115 us
    pallas_call x1, Pallas kernels, backward(): pl.pallas_call(functools.partial(backward_kernel, size, nstate, rank), in...  103 us
    pallas_call x1, Pallas kernels, place(): pl.pallas_call(functools.partial(place_kernel, sizes), grid_spec=pltpu.Pr...  10.5 us

commit v1 on v0

--- a/solution.py
+++ b/solution.py
@@ -513,6 +513,89 @@
     )(pre, act, coef, spread_by, keep, rate, rows)
 
 
+def start_send(*copy):
+    remote(*copy).start()
+
+
+class Sends:
+    def __init__(self):
+        self.sent = []
+
+    def __call__(self, *copy):
+        moving = remote(*copy)
+        moving.start()
+        self.sent.append(moving)
+
+    def wait(self):
+        for moving in self.sent:
+            moving.wait_send()
+        self.sent = []
+
+
+class Pieces:
+    def __init__(self, peers, send, sems, own_sems, index, own, view, kept=True):
+        self.peers, self.send, self.sems, self.own_sems = peers, send, sems, own_sems
+        self.index, self.own, self.view, self.kept = index, own, view, kept
+
+    def keep(self):
+        return pltpu.make_async_copy(self.own(), self.view(0), self.own_sems.at[self.index])
+
+    def give(self):
+        if self.kept:
+            self.keep().start()
+        self.send(self.own(), self.view(2), self.sems, (self.index, 0), self.peers.across)
+        self.send(self.own(), self.view(1), self.sems, (self.index, 1), self.peers.core)
+
+    def pass_on(self):
+        there = self.view(2)
+        remote(there, there, self.sems, (self.index, 0), self.peers.across).wait_recv()
+        self.send(there, self.view(3), self.sems, (self.index, 2), self.peers.core)
+
+    def come(self):
+        for k, which in ((1, 1), (3, 2)):
+            there = self.view(k)
+            remote(there, there, self.sems, (self.index, which), self.peers.core).wait_recv()
+        if self.kept:
+            self.keep().wait()
+
+    def sent_all(self):
+        for which, target in ((0, 2), (1, 1), (2, 3)):
+            there = self.view(target)
+            remote(there, there, self.sems, (self.index, which), self.peers.core).wait_send()
+
+
+class Parts:
+    def __init__(self, peers, send, sems, parts, near, far, rows):
+        self.peers, self.send, self.sems = peers, send, sems
+        self.parts, self.near, self.far, self.rows = parts, near, far, rows
+
+    def block(self, k):
+        return self.parts.at[pl.ds(k * self.rows, self.rows), :]
+
+    def start(self):
+        for i in range(2):
+            self.send(self.block(2 * i + 1), self.near.at[i], self.sems, i, self.peers.core)
+
+    def come_near(self):
+        for i in range(2):
+            there = self.near.at[i]
+            remote(there, there, self.sems, i, self.peers.core).wait_recv()
+
+    def go_far(self, here):
+        there = self.block(2)
+        there[...] = (there[...].astype(F32) + here[...].astype(F32)).astype(BF16)
+        self.send(there, self.far, self.sems, 2, self.peers.across)
+
+    def come(self):
+        remote(self.far, self.far, self.sems, 2, self.peers.across).wait_recv()
+
+    def sent_all(self):
+        for i in range(2):
+            there = self.near.at[i]
+            remote(there, there, self.sems, i, self.peers.core).wait_send()
+        remote(self.far, self.far, self.sems, 2, self.peers.across).wait_send()
+
+
 class Shares:
     def __init__(self, peers, shards, wholes, sems):
         self.peers, self.shards, self.wholes, self.sems = peers, shards, wholes, sems
@@ -572,12 +655,12 @@
     size, rank, nstate,
     entry, few, tokens, out_grad, segments, out_proj,
     few_out, masks_out, rate_out, spread_out, fold_out, normed_out, cotangent_out, tokens_all, grads_all, segments_all,
-    w_in_out, inner_out, act_out, low_out, step_low_out, coef_out, step_out, start_out, gate_out, readout_out,
+    w_in_out, inner_out, act_out, low_out, step_low_out, coef_out, step_out, states_out, gate_out, readout_out,
     gated_out, natural_out, gate_w_out, out_w_out,
     few_all, small, masks, rate, spread_by, fold_by, normed, stage, cotangent, held, seg, inner_shard, gate_shard, w_in,
     inner, act, low, part, nat, got_near, to_across, got_across, shared, step_low, coef, wide, pre, step, readout,
-    carry, start_at, gate, gated, natural, gate_w,
-    local, start_sems, gate_sems, own_sems, entry_sems, stage_sems, out_sems, seg_sems,
+    carry, states_at, gate, gated, natural, gate_w,
+    local, states_sems, gate_sems, own_sems, entry_sems, stage_sems, out_sems, seg_sems,
     ring_send, ring_recv, few_send, few_recv, rep_send, rep_recv, near_send, near_recv,
 ):
     peers = Peers(size)
@@ -625,17 +708,13 @@
     def exchange(i, own, everyone):
         send(own, of_copy(everyone, 2), rep_sems, (i, 0), peers.across)
         send(own, of_copy(everyone, 1), rep_sems, (i, 1), peers.core)
-        copy = pltpu.make_async_copy(own, of_copy(everyone, 0), own_sems.at[3 + i])
-        copy.start()
-        return copy
 
     def pass_on(i, everyone):
         far = of_copy(everyone, 2)
         remote(far, far, rep_sems, (i, 0), peers.across).wait_recv()
         send(far, of_copy(everyone, 3), rep_sems, (i, 2), peers.core)
 
-    def exchanged(i, everyone, copy):
-        copy.wait()
+    def exchanged(i, everyone):
         for k, which in ((1, 1), (3, 2)):
             there = of_copy(everyone, k)
             remote(there, there, rep_sems, (i, which), peers.core).wait_recv()
@@ -671,17 +750,21 @@
             send(source, target, few_sems, (way, number - 1), peers.ring[way])
 
     few_step(1)
-    own_tokens = exchange(0, tokens, tokens_all)
-    own_segments = exchange(2, segments, segments_all)
+    exchange(2, segments, segments_all)
+    exchange(0, tokens, tokens_all)
     own = [
         pltpu.make_async_copy(few, few_all.at[:, own_columns], own_sems.at[0]),
-        pltpu.make_async_copy(out_shard, out_w_out.at[own_rows, :], own_sems.at[1]),
+        pltpu.make_async_copy(out_shard, cotangent.at[1], own_sems.at[1]),
+        pltpu.make_async_copy(segments, seg.at[0], own_sems.at[3]),
     ]
     for copy in own:
         copy.start()
     for pick in picks[:size]:
         pick.wait()
     ring.step(0, 1)
+    own[1].wait()
+    own_out = pltpu.make_async_copy(cotangent.at[1], out_w_out.at[own_rows, :], own_sems.at[4])
+    own_out.start()
     for pick in picks[size:]:
         pick.wait()
     own_shards = [
@@ -708,14 +791,17 @@
     few_step(3)
     ring.step(0, 2)
     few_step(4)
-    exchanged(2, segments_all, own_segments)
-    numbers = pltpu.make_async_copy(segments_all, seg, seg_sems.at[0])
+    exchanged(2, segments_all)
+    others = pl.ds(1, COPIES - 1)
+    numbers = pltpu.make_async_copy(segments_all.at[others], seg.at[others], seg_sems.at[0])
     numbers.start()
     for way in range(2):
         few_come(way, half - 1) if half < 2 else None
         few_come(way, half)
     own[0].wait()
+    own[2].wait()
     numbers.wait()
+    own_out.wait()
 
     numbers = jnp.concatenate([seg[k] for k in range(COPIES)], axis=0).astype(F32)
     lane = lax.broadcasted_iota(jnp.int32, (total, LANES), 1)
@@ -736,10 +822,21 @@
         rate[n] = jnp.broadcast_to(-LOG2E * jnp.exp(small[6 + n : 7 + n, :]), (GROUP, width))
     save(rate, rate_out)
 
-    def fetch(source, t, slot):
-        return pltpu.make_async_copy(
-            source.at[:, pl.ds(pl.multiple_of(t * BLOCK, BLOCK), BLOCK), :], stage.at[slot], stage_sems.at[slot]
-        )
+    def fetch(own, everyone, t, slot):
+        these = pl.ds(pl.multiple_of(t * BLOCK, BLOCK), BLOCK)
+        others = pl.ds(batches, GROUP - batches)
+        return [
+            pltpu.make_async_copy(own.at[:, these, :], stage.at[slot, pl.ds(0, batches)], stage_sems.at[0, slot]),
+            pltpu.make_async_copy(everyone.at[others, these, :], stage.at[slot, others], stage_sems.at[1, slot]),
+        ]
+
+    def fetch_start(*what):
+        for copy in fetch(*what):
+            copy.start()
+
+    def fetch_wait(*what):
+        for copy in fetch(*what):
+            copy.wait()
 
     def weave(slot, scaled):
         for s in range(GROUP):
@@ -760,11 +857,11 @@
     def block_of(t):
         return pl.ds(pl.multiple_of(t * block_rows, block_rows), block_rows)
 
+    ring.step(0, 3)
     pass_on(0, tokens_all)
-    own_grads = exchange(1, out_grad, grads_all)
-    ring.step(0, 3)
-    exchanged(0, tokens_all, own_tokens)
-    fetch(tokens_all, 0, 0).start()
+    exchange(1, out_grad, grads_all)
+    exchanged(0, tokens_all)
+    fetch_start(tokens, tokens_all, 0, 0)
 
     @pl.loop(0, blocks)
     def _(t):
@@ -772,14 +869,14 @@
 
         @pl.when(t + 1 < blocks)
         def _():
-            fetch(tokens_all, t + 1, 1 - slot).start()
+            fetch_start(tokens, tokens_all, t + 1, 1 - slot)
 
         @pl.when(t == blocks - 2)
         def _():
             ring.step(0, 4)
             ring.step(1, 1)
 
-        fetch(tokens_all, t, slot).wait()
+        fetch_wait(tokens, tokens_all, t, slot)
         weave(slot, True)
         for k in range(held.shape[0]):
             normed[block_of(t), k * LANES : (k + 1) * LANES] = held[k].astype(BF16)
@@ -794,7 +891,7 @@
         return pltpu.make_async_copy(cotangent.at[slot], cotangent_out.at[block_of(t), :], out_sems.at[slot])
 
     def weave_grads(first, count):
-        fetch(grads_all, first, first % 2).start()
+        fetch_start(out_grad, grads_all, first, first % 2)
 
         @pl.loop(first, first + count)
         def _(t):
@@ -802,13 +899,13 @@
 
             @pl.when(t + 1 < first + count)
             def _():
-                fetch(grads_all, t + 1, 1 - slot).start()
+                fetch_start(out_grad, grads_all, t + 1, 1 - slot)
 
             @pl.when(t >= 2)
             def _():
                 cotangent_out_of(t - 2, slot).wait()
 
-            fetch(grads_all, t, slot).wait()
+            fetch_wait(out_grad, grads_all, t, slot)
             weave(slot, False)
             for k in range(held.shape[0]):
                 cotangent[slot, :, k * LANES : (k + 1) * LANES] = held[k].astype(BF16)
@@ -822,9 +919,9 @@
         cols = pl.ds(pl.multiple_of(c * chunk, chunk), chunk)
         inner[pad:, cols] = jnp.dot(normed[...], w_in[:, cols], preferred_element_type=F32)
 
-        @pl.when(c == 1)
+        @pl.when(c == 2)
         def _():
-            ring.step(2, 1)
+            ring.step(1, 2)
 
         tap = [small[taps + i : taps + i + 1, cols] for i in range(5)]
 
@@ -866,15 +963,14 @@
 
     for i in range(2):
         start(nat.at[:, pl.ds((2 * i + 1) * side_rows, side_rows), :], got_near.at[i], i, peers.core)
-    ring.step(1, 2)
     pass_on(1, grads_all)
     for i in range(2):
         come(got_near.at[i], i, peers.core)
     to_across[...] = nat[:, 2 * side_rows : 3 * side_rows, :] + got_near[1]
     start(to_across, got_across, 2, peers.across)
-    exchanged(1, grads_all, own_grads)
+    exchanged(1, grads_all)
     weave_grads(0, blocks // 2)
-    ring.step(2, 2)
+    ring.step(1, 3)
     come(got_across, 2, peers.across)
     mine = nat[:, :side_rows, :] + got_near[0] + got_across[...]
     shared[0, 0] = mine[0].astype(BF16)
@@ -909,12 +1005,17 @@
     side_bias = small[bias_row : bias_row + 1, :]
     carry[...] = jnp.zeros_like(carry)
 
-    def keep_start(t, slot):
-        return pltpu.make_async_copy(start_at.at[slot], start_out.at[t], start_sems.at[slot])
+    state_rows = nstate * GROUP
+
+    def keep_states(t, c):
+        there = pl.ds(pl.multiple_of(t * BLOCK * state_rows, BLOCK * state_rows), BLOCK * state_rows)
+        return pltpu.make_async_copy(
+            states_at.at[c % 2], states_out.at[c, there, :], states_sems.at[c % 2]
+        )
 
     @pl.loop(0, blocks)
     def _(t):
-        for tick, which, number in ((0, 1, 3), (2, 2, 3), (4, 1, 4), (6, 2, 4)):
+        for tick, which, number in ((0, 1, 4), (0, 2, 1), (4, 2, 2), (7, 2, 3)):
 
             @pl.when(t == tick)
             def _(which=which, number=number):
@@ -927,16 +1028,16 @@
         for i in range(BLOCK // 2):
             sub = slice(i * 2 * GROUP, (i + 1) * 2 * GROUP)
             step[pl.ds(base + i * 2 * GROUP, 2 * GROUP), :] = softplus(pre[sub, :] + side_bias)
-        slot = lax.rem(t, 2)
-
-        @pl.when(t >= 2)
-        def _():
-            keep_start(t - 2, slot).wait()
-
-        start_at[slot] = carry[...]
-        keep_start(t, slot).start()
         for c in range(width // chunk):
             cols = slice(c * chunk, (c + 1) * chunk)
+
+            if c >= 2:
+                keep_states(t, c - 2).wait()
+            else:
+
+                @pl.when(t > 0)
+                def _(c=c):
+                    keep_states(t - 1, c + 2).wait()
 
             def advance(i, states):
                 at = pl.ds(pl.multiple_of(base + i * GROUP, GROUP), GROUP)
@@ -949,6 +1050,8 @@
                 for n in range(nstate):
                     write = tiled(wide[here, n * LANES : (n + 1) * LANES], chunk)
                     read = tiled(wide[here, (nstate + n) * LANES : (nstate + n + 1) * LANES], chunk)
+                    row = pl.multiple_of(i * state_rows + n * GROUP, GROUP)
+                    states_at[c % 2, pl.ds(row, GROUP), :] = states[n]
                     state = jnp.exp2(drive * rate[n, :, cols]) * states[n] + write * inflow
                     out = out + read * state
                     now.append(state)
@@ -956,11 +1059,13 @@
                 return tuple(now)
 
             states = lax.fori_loop(
-                0, BLOCK, advance, tuple(carry[n, :, cols] for n in range(nstate)), unroll=4
+                0, BLOCK, advance, tuple(carry[c, n * GROUP : (n + 1) * GROUP, :] for n in range(nstate)), unroll=4
             )
             for n in range(nstate):
-                carry[n, :, cols] = states[n]
-
+                carry[c, n * GROUP : (n + 1) * GROUP, :] = states[n]
+            keep_states(t, c).start()
+
+    save(carry, states_out.at[:, pl.ds(total // GROUP * state_rows, state_rows), :])
     save(step, step_out)
     save(readout, readout_out)
 
@@ -979,6 +1084,10 @@
         @pl.when(c >= 2)
         def _():
             keep_gate(c - 2, slot).wait()
+
+        @pl.when(c == 2)
+        def _():
+            ring.step(2, 4)
 
         gate[slot] = jnp.dot(normed[...], gate_w[:, cols], preferred_element_type=F32)
         keep_gate(c, slot).start()
@@ -1000,13 +1109,12 @@
 
     save(gated, gated_out)
     save(natural, natural_out)
-    own[1].wait()
     ring.finish(2)
     ring.sent_all()
     for moving in sent:
         moving.wait_send()
     for slot in range(2):
-        keep_start(blocks - 2 + slot, slot).wait()
+        keep_states(blocks - 1, width // chunk - 2 + slot).wait()
         keep_gate(width // chunk - 2 + slot, slot).wait()
         cotangent_out_of(blocks - 2 + slot, slot).wait()
     for copy in saved:
@@ -1049,7 +1157,7 @@
         step_low=thin,
         coef=thin,
         step=full,
-        starts=shape((blocks,) + state.shape, F32),
+        states=shape((width // 256, (length + 1) * nstate * GROUP, 256), F32),
         gate=full,
         readout=full,
         gated=low,
@@ -1088,14 +1196,14 @@
         shape((BLOCK * GROUP, width), F32),
         full,
         full,
-        state,
-        shape((2,) + state.shape, F32),
+        shape((width // 256, nstate * GROUP, 256), F32),
+        shape((2, BLOCK * nstate * GROUP, 256), F32),
         shape((2, total, 256), F32),
         low,
         low,
         weights,
     ]
-    sems = [(20,), (2,), (2,), (7,), (2 * size,), (2,), (2,), (1,)]
+    sems = [(20,), (2,), (2,), (7,), (2 * size,), (2, 2), (2,), (1,)]
     sems += [(3, 2, half, 2)] * 2 + [(2, half)] * 2 + [(3, 3)] * 2 + [(6,)] * 2
     results = pl.pallas_call(
         functools.partial(forward_kernel, size, rank, nstate),
@@ -1150,18 +1258,19 @@
                 if c in self.chunks(way, step):
                     self.copy(which, way, step, c, self.source(which, way, step, c)).start()
 
-    def finish(self):
+    def finish(self, which):
         last = self.peers.half
+        for c in range(2):
+            total = self.own(which, 0, last + 1, c)[...].astype(F32)
+            for way in range(2):
+                self.copy(which, way, last, c).wait_recv()
+                there = self.held[which].at[way, last - 1, self.rows(which, c), :]
+                total = total + there[...].astype(F32)
+            self.totals[which][self.rows(which, c), :] = total.astype(BF16)
+
+    def sent_all(self):
         for which in range(2):
-            for c in range(2):
-                total = self.own(which, 0, last + 1, c)[...].astype(F32)
-                for way in range(2):
-                    self.copy(which, way, last, c).wait_recv()
-                    there = self.held[which].at[way, last - 1, self.rows(which, c), :]
-                    total = total + there[...].astype(F32)
-                self.totals[which][self.rows(which, c), :] = total.astype(BF16)
-        for which in range(2):
-            for step in range(1, last + 1):
+            for step in range(1, self.peers.half + 1):
                 for way in range(2):
                     for c in self.chunks(way, step):
                         self.copy(which, way, step, c).wait_send()
@@ -1313,13 +1422,14 @@
 
 def backward_kernel(
     size, nstate, rank,
-    gated_in, cotangent_in, w_out, readout_in, gate_in, normed_in, step_in, act_in, coef_in, starts_in, masks_in, rate_in,
-    spread_in, fold_in, few_in,
-    natural_out, pre_low_out, direct_out, coef_grad_out, sums_out, out_total, gate_total,
+    gated_in, cotangent_in, w_out, readout_in, gate_in, normed_in, step_in, act_in, coef_in, states_in, masks_in, rate_in,
+    spread_in, fold_in, few_in, gated_natural_in,
+    natural_out, pre_low_out, direct_out, coef_grad_out, sums_out, out_pieces, out_own, out_near, out_far, gate_total,
     gated, cotangent, out_w, normed, out_wgrad, gate_wgrad, out_held, gate_held, gate_grad, natural, grad, nat,
-    step_at, act_at, start_at, wide, states_all, decays, parts, sizes, sums, carry, coef, spread_by, fold_by, rate, keep, few,
-    coef_grad,
-    load_sems, tile_sems, block_sems, save_sems, block_saves, ring_send, ring_recv,
+    step_at, act_at, states_at, wide, parts, sizes, sums, carry, coef, spread_by, fold_by, rate, keep, few,
+    coef_grad, out_total,
+    load_sems, tile_sems, block_sems, states_sems, save_sems, block_saves, ring_send, ring_recv, part_send, part_recv,
+    piece_send, piece_recv, own_sem,
 ):
     peers = Peers(size)
     total, width = gated.shape
@@ -1352,17 +1462,25 @@
 
     def tile_copies(c, slot):
         cols = pl.ds(pl.multiple_of(c * chunk, chunk), chunk)
-        there = pl.ds(pl.multiple_of(slot * total, total), total)
         return [
-            pltpu.make_async_copy(gate_in.at[:, cols], decays.at[there, :], tile_sems.at[0, slot]),
-            pltpu.make_async_copy(readout_in.at[:, cols], states_all.at[there, :], tile_sems.at[1, slot]),
+            pltpu.make_async_copy(
+                ref.at[:, cols], states_at.at[slot, pl.ds(i * total, total), :], tile_sems.at[i, slot]
+            )
+            for i, ref in enumerate((gate_in, readout_in))
         ]
 
     for copy in tile_copies(0, 0):
         copy.start()
     peers.meet()
     ring = Guests(
-        peers, (out_wgrad, gate_wgrad), None, (out_held, gate_held), (ring_send, ring_recv)
+        peers, (out_wgrad, gate_wgrad), (out_total, gate_total), (out_held, gate_held), (ring_send, ring_recv),
+    )
+    out_parts = cotangent
+    out_sum = Parts(
+        peers, start_send, (part_send, part_recv), out_parts, out_near, out_far, total // COPIES
+    )
+    pieces = Pieces(
+        peers, start_send, (piece_send, piece_recv), own_sem, 0, lambda: out_total, lambda k: out_pieces.at[k],
     )
     loads["gated"].wait()
     loads["cotangent"].wait()
@@ -1400,8 +1518,9 @@
         def _(i):
             start = pl.multiple_of(i * rows, rows)
             at = pl.ds(start, rows)
-            there = pl.ds(pl.multiple_of(slot * total + start, rows), rows)
-            gate, readout, value = decays[there, :], states_all[there, :], grad[at, cols]
+            gate = states_at[slot, at, :]
+            readout = states_at[slot, pl.ds(total + start, rows), :]
+            value = grad[at, cols]
             sig = sigmoid(gate)
             grad[at, cols] = value * (gate * sig)
             value = value * readout * (sig * (1.0 + gate * (1.0 - sig)))
@@ -1423,8 +1542,22 @@
         return [
             pltpu.make_async_copy(step_in.at[these, :], step_at.at[slot], block_sems.at[0, slot]),
             pltpu.make_async_copy(act_in.at[these, :], act_at.at[slot], block_sems.at[1, slot]),
-            pltpu.make_async_copy(starts_in.at[t], start_at.at[slot], block_sems.at[2, slot]),
         ]
+
+    state_rows = nstate * GROUP
+
+    def states_copy(t, c):
+        there = pl.ds(pl.multiple_of(t * BLOCK * state_rows, BLOCK * state_rows), (BLOCK + 1) * state_rows)
+        slot = states_slot(t, c)
+        return pltpu.make_async_copy(states_in.at[c, there, :], states_at.at[slot], states_sems.at[slot])
+
+    slots, ahead = 3, 2
+
+    def states_slot(t, c):
+        return lax.rem((blocks - 1 - t) * (width // chunk) + c, slots)
+
+    for c in range(ahead):
+        states_copy(blocks - 1, c).start()
 
     for copy in block_copies(blocks - 1, (blocks - 1) % 2):
         copy.start()
@@ -1437,6 +1570,7 @@
         gate_wgrad[:, :, cols] = value.astype(BF16).reshape(size, -1, chunk)
 
     ring.step(1, 1)
+    load("natural", gated_natural_in, gate_grad)
     for name in ("coef", "spread", "fold", "rate", "keep", "few"):
         loads[name].wait()
     pre_low = gated
@@ -1445,6 +1579,13 @@
     carry[...] = jnp.zeros_like(carry)
     sums[...] = jnp.zeros_like(sums)
 
+    def near_copy():
+        return pltpu.make_async_copy(
+            out_near.at[1], normed.at[pl.ds(0, total // COPIES), :], own_sem.at[1]
+        )
+
+    loads["natural"].wait()
+
     def fold(value):
         out = value[:, :LANES]
         for k in range(1, chunk // LANES):
@@ -1468,6 +1609,28 @@
             def _(which=which, number=number):
                 ring.step(which, number)
 
+        @pl.when(turn == 1)
+        def _():
+            out_sum.start()
+
+        @pl.when(turn == 2)
+        def _():
+            near_copy().wait()
+            out_sum.go_far(normed.at[pl.ds(0, total // COPIES), :])
+
+        @pl.when(turn == 5)
+        def _():
+            ring.finish(0)
+            pieces.give()
+
+        @pl.when(turn == 0)
+        def _():
+            @pl.loop(0, model // chunk)
+            def _(i):
+                cols = pl.ds(pl.multiple_of(i * chunk, chunk), chunk)
+                value = jnp.dot(gate_grad[...], out_w[:, cols], preferred_element_type=F32)
+                out_parts[:, cols] = value.astype(BF16)
+
         @pl.when(t > 0)
         def _():
             for copy in block_copies(t - 1, 1 - slot):
@@ -1482,28 +1645,19 @@
         for c in range(width // chunk):
             cols = slice(c * chunk, (c + 1) * chunk)
 
-            def entry(i, n):
-                return pl.ds(pl.multiple_of((i * nstate + n) * GROUP, GROUP), GROUP)
-
-            def advance(i, states):
-                here = at_time(i)
-                at = pl.ds(pl.multiple_of(base + i * GROUP, GROUP), GROUP)
-                step = step_at[slot, here, cols]
-                drive = jnp.where(tiled(keep[at, :], chunk) > 0.5, step, FAR)
-                inflow = step * act_at[slot, here, cols]
-                now = []
-                for n in range(nstate):
-                    write = tiled(wide[here, n * LANES : (n + 1) * LANES], chunk)
-                    decay = jnp.exp2(drive * rate[n, :, cols])
-                    decays[entry(i, n), :] = decay
-                    states_all[entry(i, n), :] = states[n]
-                    now.append(decay * states[n] + write * inflow)
-                return tuple(now)
-
-            start = tuple(start_at[slot, n, :, cols] for n in range(nstate))
-            states = lax.fori_loop(0, BLOCK, advance, start, unroll=2)
-            for n in range(nstate):
-                states_all[entry(BLOCK, n), :] = states[n]
+            if c + ahead < width // chunk:
+                states_copy(t, c + ahead).start()
+            else:
+
+                @pl.when(t > 0)
+                def _(c=c):
+                    states_copy(t - 1, c + ahead - width // chunk).start()
+
+            states_copy(t, c).wait()
+
+            def state_at(i, n):
+                row = pl.multiple_of(i * state_rows + n * GROUP, GROUP)
+                return states_at[states_slot(t, c), pl.ds(row, GROUP), :]
 
             def retreat(i, carried):
                 i = BLOCK - 1 - i
@@ -1511,19 +1665,21 @@
                 at = pl.ds(pl.multiple_of(base + i * GROUP, GROUP), GROUP)
                 step, act, flow = step_at[slot, here, cols], act_at[slot, here, cols], grad[at, cols]
                 inflow = step * act
+                drive = jnp.where(tiled(keep[at, :], chunk) > 0.5, step, FAR)
                 size_grad, direct = jnp.zeros_like(step), jnp.zeros_like(step)
                 now = []
                 for n in range(nstate):
                     tile_w = slice(n * LANES, (n + 1) * LANES)
                     tile_r = slice((nstate + n) * LANES, (nstate + n + 1) * LANES)
                     state_grad = tiled(wide[here, tile_r], chunk) * flow + carried[n]
-                    passed = decays[entry(i, n), :] * state_grad
-                    through = passed * states_all[entry(i, n), :]
-                    size_grad = size_grad + rate[n, :, cols] * through
+                    power = drive * rate[n, :, cols]
+                    passed = jnp.exp2(power) * state_grad
+                    through = power * (passed * state_at(i, n))
+                    size_grad = size_grad + through
                     direct = direct + state_grad * tiled(wide[here, tile_w], chunk)
-                    sums[n, :, cols] += step * through
+                    sums[n, :, cols] += through
                     write_part = fold(state_grad * inflow)
-                    read_part = fold(flow * states_all[entry(i + 1, n), :])
+                    read_part = fold(flow * state_at(i + 1, n))
                     if c == 0:
                         parts[here, tile_w] = write_part
                         parts[here, tile_r] = read_part
@@ -1531,13 +1687,13 @@
                         parts[here, tile_w] += write_part
                         parts[here, tile_r] += read_part
                     now.append(passed)
-                sizes[here, cols] = LN2 * size_grad + act * direct
+                sizes[here, cols] = LN2 * size_grad / jnp.maximum(step, 1e-30) + act * direct
                 grad[at, cols] = step * direct + skip_row[:, cols] * flow
                 sums[nstate, :, cols] += flow * act
                 return tuple(now)
 
             start = tuple(carry[n, :, cols] for n in range(nstate))
-            carried = lax.fori_loop(0, BLOCK, retreat, start, unroll=2)
+            carried = lax.fori_loop(0, BLOCK, retreat, start, unroll=4)
             for n in range(nstate):
                 carry[n, :, cols] = carried[n]
 
@@ -1549,18 +1705,28 @@
         for i in range(1, BLOCK):
             tally = tally + pre_grad[i * GROUP : (i + 1) * GROUP]
         sums[nstate + 1] += tally
-        high = parts[...].astype(BF16)
-        low = (parts[...] - high.astype(F32)).astype(BF16)
-        coef_grad[these, :] = jnp.dot(high, fold_by[...], preferred_element_type=F32) + jnp.dot(
-            low, fold_by[...], preferred_element_type=F32
+        coef_grad[these, :] = jnp.dot(
+            parts[...].astype(BF16), fold_by[...], preferred_element_type=F32
         )
+
+        @pl.when(turn == 1)
+        def _():
+            out_sum.come_near()
+            near_copy().start()
+
         for copy in block_keeps(t):
             copy.start()
 
     save(coef_grad, coef_grad_out)
     save(sums, sums_out)
-    ring.totals = (out_total, gate_total)
-    ring.finish()
+    save(out_sum.block(0), out_own)
+    pieces.pass_on()
+    ring.finish(1)
+    pieces.come()
+    out_sum.come()
+    ring.sent_all()
+    out_sum.sent_all()
+    pieces.sent_all()
     for t in range(blocks):
         for copy in block_keeps(t):
             copy.wait()
@@ -1569,7 +1735,7 @@
 
 
 def backward(size, nstate, rank, arrays):
-    gated, cotangent, w_out, readout, gate, normed, step, act, coef, starts, masks, rate, spread_by, fold_by, few = arrays
+    (gated, cotangent, w_out, readout, gate, normed, step, act, coef, states, masks, rate, spread_by, fold_by, few) = arrays[:15]
     total, width = gated.shape
     model = normed.shape[1]
     inside, anywhere = pl.BlockSpec(memory_space=pltpu.VMEM), pl.BlockSpec(memory_space=pl.ANY)
@@ -1597,10 +1763,8 @@
         shape((2, total, LANES), F32),
         block,
         block,
-        shape((2,) + state.shape, F32),
+        shape((3, (BLOCK + 1) * nstate * GROUP, 256), F32),
         wide,
-        shape(((BLOCK + 1) * nstate * GROUP, 256), F32),
-        shape((BLOCK * nstate * GROUP, 256), F32),
         wide,
         shape((BLOCK * GROUP, width), F32),
         tally,
@@ -1612,14 +1776,20 @@
         thin,
         shape((few.shape[0] - 2 * rank - 2 * nstate, width), BF16),
         thin,
+        shape(out_unit, BF16),
     ]
     blocks = total // (BLOCK * GROUP)
-    sems = [(10,), (2, 2), (3, 2), (3,), (2, blocks), (2, 2, half, 2), (2, 2, half, 2)]
+    sems = [(11,), (2, 2), (2, 2), (3,), (4,), (2, blocks), (2, 2, half, 2), (2, 2, half, 2)]
+    sems += [(3,), (3,), (1, 3), (1, 3), (2,)]
+    part = shape((total // COPIES, model), BF16)
     return pl.pallas_call(
         functools.partial(backward_kernel, size, nstate, rank),
         in_specs=[anywhere] * len(arrays),
-        out_specs=[anywhere] * 5 + [inside] * 2,
-        out_shape=[low, low, full, thin, tally, shape(out_unit, BF16), shape(gate_unit, BF16)],
+        out_specs=[anywhere] * 9 + [inside],
+        out_shape=[
+            low, low, full, thin, tally, shape((COPIES,) + out_unit, BF16), part, shape((2,) + part.shape, BF16), part,
+            shape(gate_unit, BF16),
+        ],
         scratch_shapes=[pltpu.VMEM(x.shape, x.dtype) for x in scratch] + [dma(n) for n in sems],
         compiler_params=pltpu.CompilerParams(
             collective_id=3, has_side_effects=True, vmem_limit_bytes=62 * 1024 * 1024
@@ -1632,12 +1802,11 @@
 def finish_kernel(
     size, rank, nstate,
     pre_low_in, coef_in, direct_in, inner_in, act_low_in, step_low_in, masks_in, few_in, normed_in, w_inner, w_gate,
-    gate_grad_in, gated_in, w_out, sums_in, out_total, gate_total,
-    inner_pieces, gate_pieces, out_pieces, small_pieces, out_sum, norm_sum,
+    gate_grad_in, sums_in, gate_total,
+    inner_pieces, gate_pieces, norm_own, norm_near, norm_far, small_pieces,
     pre_low, part, nat, got_near, to_across, got_across, shared, low_grad, act_low, step_low, masks, few, normed, gate_grad,
-    gated, inner, direct, grad, wgrad, held, small, small_low, small_held, out_w, out_parts,
-    out_pair, norm_pair, out_far, norm_far, w_tiles, total_at, sums,
-    load_sems, tile_sems, w_sems, near_send, near_recv, pair_send, pair_recv, ring_send, ring_recv, few_send, few_recv,
+    inner_grad, inner, direct, grad, wgrad, held, small, small_low, small_held, norm_parts, near_at, w_tiles, total_at, gate_own, sums,
+    load_sems, tile_sems, w_sems, near_send, near_recv, part_send, part_recv, ring_send, ring_recv, few_send, few_recv,
     piece_send, piece_recv, own_sems,
 ):
     peers = Peers(size)
@@ -1650,16 +1819,11 @@
     chunk, rows, pad = 256, 64, 3 * GROUP
     tiles = width // chunk
     slab = held.shape[2]
-    sent, loads = [], {}
+    send, loads = Sends(), {}
 
     def load(name, source, target):
         loads[name] = pltpu.make_async_copy(source, target, load_sems.at[len(loads)])
         loads[name].start()
-
-    def send(*copy):
-        moving = remote(*copy)
-        moving.start()
-        sent.append(moving)
 
     def tile_copies(c, slot):
         cols = slice(c * chunk, (c + 1) * chunk)
@@ -1672,15 +1836,39 @@
     load("few", few_in, few)
     load("coef", coef_in, part.at[1])
     load("step", step_low_in, step_low)
-    load("gated", gated_in, gated)
-    load("out_w", w_out, out_w)
+    load("gate", gate_grad_in, gate_grad)
+    load("total", gate_total, gate_own)
     load("act", act_low_in, act_low)
     load("masks", masks_in, masks.at[:, pl.ds(0, total), :])
     load("normed", normed_in, normed)
     load("sums", sums_in, sums)
-    load("gate", gate_grad_in, gate_grad)
     for copy in tile_copies(0, 0):
         copy.start()
+    w_count = model // chunk
+
+    def w_copy(w, n, slot):
+        these = pl.ds(pl.multiple_of(n * chunk, chunk), chunk)
+        return pltpu.make_async_copy(w.at[these, :], w_tiles.at[slot], w_sems.at[slot])
+
+    def norm_tiles(w, left, first, count, add):
+        @pl.loop(first, first + count)
+        def _(n):
+            slot = lax.rem(n, 2)
+
+            @pl.when(n + 1 < w_count)
+            def _():
+                w_copy(w, n + 1, 1 - slot).start()
+
+            w_copy(w, n, slot).wait()
+            cols = pl.ds(pl.multiple_of(n * chunk, chunk), chunk)
+            value = lax.dot_general(
+                left[...], w_tiles[slot], (((1,), (1,)), ((), ())), preferred_element_type=F32
+            )
+            if add:
+                value = value + norm_parts[:, cols].astype(F32)
+            norm_parts[:, cols] = value.astype(BF16)
+
+    w_copy(w_gate, 0, 0).start()
     peers.meet()
 
     near = (near_send, near_recv)
@@ -1701,7 +1889,8 @@
             nat[j, s * length : (s + 1) * length, :] = part[j, pl.ds(s, length, stride=GROUP), :]
     for i in range(2):
         send(nat.at[:, pl.ds((2 * i + 1) * quarter, quarter), :], got_near.at[i], near, i, peers.core)
-    near_sends = list(sent)
+    near_sends = Sends()
+    near_sends.sent, send.sent = send.sent, []
     loads["step"].wait()
     small[first_stride : first_stride + rank, :] = lax.dot_general(
         step_low[...], pre_low[...], (((0,), (0,)), ((), ())), preferred_element_type=F32
@@ -1710,29 +1899,21 @@
         come(got_near.at[i], i, peers.core)
     to_across[...] = nat[:, 2 * quarter : 3 * quarter, :] + got_near[1]
     send(to_across, got_across, near, 2, peers.across)
-    loads["gated"].wait()
-    loads["out_w"].wait()
-
-    def out_tiles(first, count):
-        @pl.loop(first, first + count)
-        def _(c):
-            cols = pl.ds(pl.multiple_of(c * chunk, chunk), chunk)
-            out_parts[:, cols] = jnp.dot(gated[...], out_w[:, cols], preferred_element_type=F32).astype(BF16)
-
-    out_tiles(0, model // chunk // 2)
+    loads["gate"].wait()
+    norm_tiles(w_gate, gate_grad, 0, w_count // 2, False)
     come(got_across, 2, peers.across)
     mine = nat[:, :quarter, :] + got_near[0] + got_across[...]
     for j in range(2):
         shared[0, j] = mine[j].astype(BF16)
     send(shared.at[0], shared.at[2], near, 3, peers.across)
     send(shared.at[0], shared.at[1], near, 4, peers.core)
-    out_tiles(model // chunk // 2, model // chunk // 2)
+    norm_tiles(w_gate, gate_grad, w_count // 2, w_count - w_count // 2, False)
+    w_copy(w_inner, 0, 0).start()
     come(shared.at[2], 3, peers.across)
     send(shared.at[2], shared.at[3], near, 5, peers.core)
     come(shared.at[1], 4, peers.core)
     come(shared.at[3], 5, peers.core)
-    for copy in near_sends:
-        copy.wait_send()
+    near_sends.wait()
     for k in range(COPIES):
         for b in range(batches):
             for j in range(2):
@@ -1742,47 +1923,14 @@
     for j in range(2):
         low_grad[j] = part[j].astype(BF16)
 
-    pair_sems, piece_sems = (pair_send, pair_recv), (piece_send, piece_recv)
-    keeps = []
-
-    def of_copy(ref, k):
-        return ref.at[pl.ds(k * quarter, quarter), :]
-
-    def exchange(index, parts, pair):
-        for i in range(2):
-            send(of_copy(parts, 2 * i + 1), pair.at[i], pair_sems, 3 * index + i, peers.core)
-
-    def exchange_far(index, parts, pair, far):
-        for i in range(2):
-            remote(pair.at[i], pair.at[i], pair_sems, 3 * index + i, peers.core).wait_recv()
-        there = of_copy(parts, 2)
-        there[...] = (there[...].astype(F32) + pair[1].astype(F32)).astype(BF16)
-        send(there, far, pair_sems, 3 * index + 2, peers.across)
-
-    def exchanged(index, parts, pair, far):
-        remote(far, far, pair_sems, 3 * index + 2, peers.across).wait_recv()
-        return of_copy(parts, 0)[...].astype(F32) + pair[0].astype(F32) + far[...].astype(F32)
-
-    def give(index, own, pieces):
-        keeps.append(pltpu.make_async_copy(own, pieces[0], own_sems.at[index]))
-        keeps[-1].start()
-        send(own, pieces[2], piece_sems, (index, 0), peers.across)
-        send(own, pieces[1], piece_sems, (index, 1), peers.core)
-
-    def pass_on(index, pieces):
-        remote(pieces[2], pieces[2], piece_sems, (index, 0), peers.across).wait_recv()
-        send(pieces[2], pieces[3], piece_sems, (index, 2), peers.core)
-
-    def given(index, pieces):
-        for k, which in ((1, 1), (3, 2)):
-            remote(pieces[k], pieces[k], piece_sems, (index, which), peers.core).wait_recv()
-
-    def every(ref, *at):
-        return [ref.at[(k, *at)] for k in range(COPIES)]
-
-    exchange(0, out_parts, out_pair)
-    give(0, out_total, every(out_pieces))
-    give(1, gate_total, every(gate_pieces))
+    piece_sems = (piece_send, piece_recv)
+
+    def pieces_of(index, own, view):
+        return Pieces(peers, send, piece_sems, own_sems, index, own, view)
+
+    gate_all = pieces_of(0, lambda: gate_own, lambda k: gate_pieces.at[k])
+    loads["total"].wait()
+    gate_all.give()
 
     loads["act"].wait()
     for j, n in ((0, rank), (1, 2 * nstate)):
@@ -1791,7 +1939,7 @@
         )
         small[j * rank : j * rank + n, :] = weights[:n]
 
-    inner_grad, natural = gated, pre_low
+    natural = pre_low
     loads["masks"].wait()
     loads["normed"].wait()
     masks[:, total:, :] = jnp.zeros((3, pad, LANES), F32)
@@ -1905,19 +2053,14 @@
             normed[...], inner_grad[:, cols], (((0,), (0,)), ((), ())), preferred_element_type=F32
         ).astype(BF16)
         ring_step(1, c)
-        if c == 1:
-            exchange_far(0, out_parts, out_pair, out_far)
         if c >= 2:
             ring_step(2, c - 2)
 
     loads["sums"].wait()
     at = first_tap + 5
     small[at : at + 1, :] = jnp.sum(sums[nstate + 1], axis=0, keepdims=True)
-    decays = few[first_tap : first_tap + 32, :].astype(F32)
     for n in range(nstate):
-        small[at + 1 + n : at + 2 + n, :] = -jnp.exp(decays[6 + n : 7 + n]) * jnp.sum(
-            sums[n], axis=0, keepdims=True
-        )
+        small[at + 1 + n : at + 2 + n, :] = LN2 * jnp.sum(sums[n], axis=0, keepdims=True)
     at = at + 1 + nstate
     small[at : at + 1, :] = jnp.sum(sums[nstate], axis=0, keepdims=True)
     small[at + 1 :, :] = jnp.zeros((small.shape[0] - at - 1, width), F32)
@@ -1953,72 +2096,45 @@
                     source[...] = (source[...].astype(F32) + small_low[:, columns].astype(F32)).astype(BF16)
             send(source, few_landing(way, step), few_sems, (way, step - 1), peers.ring[way])
 
-    loads["gate"].wait()
-    norm_parts = out_w
-
-    def w_copies(n, slot):
-        these = pl.ds(pl.multiple_of(n * chunk, chunk), chunk)
-        return [
-            pltpu.make_async_copy(w.at[these, :], w_tiles.at[slot, i], w_sems.at[i, slot])
-            for i, w in enumerate((w_inner, w_gate))
-        ]
-
-    w_count = model // chunk
-
-    def norm_tiles(first, count):
-        @pl.loop(first, first + count)
-        def _(n):
-            slot = lax.rem(n, 2)
-
-            @pl.when(n + 1 < w_count)
-            def _():
-                for copy in w_copies(n + 1, 1 - slot):
-                    copy.start()
-
-            for copy in w_copies(n, slot):
-                copy.wait()
-            nt = (((1,), (1,)), ((), ()))
-            value = lax.dot_general(natural[...], w_tiles[slot, 0], nt, preferred_element_type=F32)
-            value += lax.dot_general(gate_grad[...], w_tiles[slot, 1], nt, preferred_element_type=F32)
-            norm_parts[:, pl.ds(pl.multiple_of(n * chunk, chunk), chunk)] = value.astype(BF16)
-
+    norm_sum = Parts(peers, send, (part_send, part_recv), norm_parts, norm_near, norm_far, quarter)
     few_step(1)
-    for copy in w_copies(0, 0):
-        copy.start()
-    for i in range(2):
-        norm_tiles(i, 1)
-        ring_step(2, 2 + i)
+    norm_tiles(w_inner, natural, 0, w_count, True)
+    norm_sum.start()
+    ring_step(2, 2)
+    ring_step(2, 3)
+    ring_step(3, 0)
+    norm_sum.come_near()
+    near_copy = pltpu.make_async_copy(norm_near.at[1], near_at, w_sems.at[2])
+    near_copy.start()
+    ring_step(3, 1)
+    near_copy.wait()
+    norm_sum.go_far(near_at)
     few_step(2)
-    for i in range(4):
-        norm_tiles(2 + i, 1)
-        ring_step(3, i)
+    ring_step(3, 2)
+    ring_step(3, 3)
     few_step(3)
-    norm_tiles(6, w_count - 6)
     own_rows = block_rows(peers.member)
     owns = [
-        pltpu.make_async_copy(w_inner.at[own_rows, :], w_tiles.at[0, 0], w_sems.at[0, 0]),
-        pltpu.make_async_copy(w_gate.at[own_rows, :], w_tiles.at[0, 1], w_sems.at[1, 0]),
-        pltpu.make_async_copy(gate_total, w_tiles.at[1, 0], w_sems.at[0, 1]),
+        pltpu.make_async_copy(w_inner.at[own_rows, :], w_tiles.at[0], w_sems.at[0]),
+        pltpu.make_async_copy(w_gate.at[own_rows, :], w_tiles.at[1], w_sems.at[1]),
+        pltpu.make_async_copy(norm_sum.block(0), norm_own, w_sems.at[3]),
     ]
     for copy in owns:
         copy.start()
-    exchange(1, norm_parts, norm_pair)
-    ring_step(4, 0)
-    ring_step(4, 1)
-    exchange_far(1, norm_parts, norm_pair, norm_far)
-    ring_step(4, 2)
-    ring_step(4, 3)
+    for c in range(tiles):
+        ring_step(4, c)
     few_step(4)
-    for index, pieces in ((0, out_pieces), (1, gate_pieces)):
-        pass_on(index, every(pieces))
-    out_sum[...] = exchanged(0, out_parts, out_pair, out_far)
+    gate_all.pass_on()
 
     def cols_of(c):
         return slice(c * chunk, (c + 1) * chunk)
 
-    def inner_views(c):
-        return [inner_pieces.at[k, :, cols_of(c)] for k in range(COPIES)]
-
+    inner_all = [
+        pieces_of(
+            1 + c, lambda c=c: total_at.at[:, cols_of(c)], lambda k, c=c: inner_pieces.at[k, :, cols_of(c)]
+        )
+        for c in range(tiles)
+    ]
     own_block = block_rows(peers.member)
     for c in range(tiles):
         for way in range(2):
@@ -2027,7 +2143,7 @@
         for way in range(2):
             value = value + held[way, half - 1, :, cols_of(c)].astype(F32)
         total_at[:, cols_of(c)] = value.astype(BF16)
-        give(3 + c, total_at.at[:, cols_of(c)], inner_views(c))
+        inner_all[c].give()
     for way in range(2):
         few_arrive(way, half)
     value = small_low[:, few_columns(peers.member)].astype(F32)
@@ -2037,8 +2153,8 @@
     small_total[...] = value.astype(BF16)
     for copy in owns:
         copy.wait()
-    value = total_at[...].astype(F32) * w_tiles[0, 0].astype(F32)
-    value = value + w_tiles[1, 0].astype(F32) * w_tiles[0, 1].astype(F32)
+    value = total_at[...].astype(F32) * w_tiles[0].astype(F32)
+    value = value + gate_own[...].astype(F32) * w_tiles[1].astype(F32)
     high = value.astype(BF16)
     low = (value - high.astype(F32)).astype(BF16)
     ones = jnp.ones((GROUP, width), BF16)
@@ -2052,36 +2168,30 @@
     for i in range(slab // LANES):
         last = jnp.where(line == gain_at + i, value[0:1, i * LANES : (i + 1) * LANES], last)
     small_total[gain_at - gain_at % 16 :, :] = last.astype(BF16)
-    send(small_total, small_pieces.at[2], piece_sems, (2, 0), peers.across)
-    send(small_total, small_pieces.at[1], piece_sems, (2, 1), peers.core)
-    norm_sum[...] = exchanged(1, norm_parts, norm_pair, norm_far)
-    for c in range(tiles):
-        pass_on(3 + c, inner_views(c))
-    pass_on(2, every(small_pieces))
-    for index, pieces in ((0, every(out_pieces)), (1, every(gate_pieces)), (2, every(small_pieces))):
-        given(index, pieces)
-    for c in range(tiles):
-        given(3 + c, inner_views(c))
-    for copy in keeps:
-        copy.wait()
-    for moving in sent[len(near_sends) :]:
-        moving.wait_send()
+    small_all = Pieces(
+        peers, send, piece_sems, None, 1 + tiles, lambda: small_total, lambda k: small_pieces.at[k], False
+    )
+    small_all.give()
+    for pieces in (*inner_all, small_all):
+        pieces.pass_on()
+    norm_sum.come()
+    for pieces in (gate_all, *inner_all, small_all):
+        pieces.come()
+    send.wait()
 
 
 def finish(size, rank, nstate, arrays, small_rows):
     (pre_low, coef, direct, inner, act_low, step_low, masks, few, normed) = arrays[:9]
     total, width = pre_low.shape
     model = normed.shape[1]
-    out_total, gate_total = arrays[-2:]
+    sums, gate_total = arrays[-2:]
     slab = gate_total.shape[0]
     quarter, half = total // COPIES, size // 2
     inside, anywhere = pl.BlockSpec(memory_space=pltpu.VMEM), pl.BlockSpec(memory_space=pl.ANY)
     shape, dma = jax.ShapeDtypeStruct, pltpu.SemaphoreType.DMA
     low = shape((total, width), BF16)
     wide = shape((total, model), BF16)
-    pair = shape((2, quarter, model), BF16)
-    far = shape((quarter, model), BF16)
-    sums = arrays[-3]
+    part = shape((quarter, model), BF16)
     padded = total + 3 * GROUP
     scratch = [
         low,
@@ -2107,30 +2217,27 @@
         shape((small_rows, width), F32),
         shape((small_rows, width), BF16),
         shape((2, half, small_rows, LANES), BF16),
-        shape((max(width, total), model), BF16),
         wide,
-        pair,
-        pair,
-        far,
-        far,
-        shape((2, 2, 256, width), BF16),
+        part,
+        shape((2, 256, width), BF16),
+        shape((slab, width), BF16),
         shape((slab, width), BF16),
         shape(sums.shape, F32),
     ]
     tiles = width // 256
-    sems = [(11,), (2, 2), (2, 2)] + [(6,)] * 2 + [(6,)] * 2 + [(2, half, tiles)] * 2 + [(2, half)] * 2
-    sems += [(3 + tiles, 3)] * 2 + [(3 + tiles,)]
+    sems = [(10,), (2, 2), (4,)] + [(6,)] * 2 + [(3,)] * 2 + [(2, half, tiles)] * 2 + [(2, half)] * 2
+    sems += [(2 + tiles, 3)] * 2 + [(1 + tiles,)]
     return pl.pallas_call(
         functools.partial(finish_kernel, size, rank, nstate),
         in_specs=[anywhere] * len(arrays),
-        out_specs=[anywhere] * 3 + [inside] * 3,
+        out_specs=[anywhere] * 5 + [inside],
         out_shape=[
             shape((COPIES, slab, width), BF16),
             shape((COPIES, slab, width), BF16),
-            shape((COPIES,) + out_total.shape, BF16),
+            part,
+            shape((2,) + part.shape, BF16),
+            part,
             shape((COPIES, small_rows, LANES), BF16),
-            shape((quarter, model), F32),
-            shape((quarter, model), F32),
         ],
         scratch_shapes=[pltpu.VMEM(x.shape, x.dtype) for x in scratch] + [dma(n) for n in sems],
         compiler_params=pltpu.CompilerParams(
@@ -2142,7 +2249,8 @@
 
 
 def place_kernel(
-    sizes, copy_ref, inner_ref, gate_ref, out_ref, small_ref, out_sum_ref, norm_ref, tokens_ref, grads_ref, few_ref,
+    sizes, copy_ref, inner_ref, gate_ref, out_ref, small_ref, out_own, out_near, out_far, norm_own, norm_near, norm_far,
+    tokens_ref, grads_ref, few_ref,
     entry_ref, out_proj_ref, select_ref, stride_ref, taps_ref, decay_ref, rows_ref, block_out_ref, input_grad_ref,
 ):
     copy = copy_ref[0]
@@ -2174,7 +2282,8 @@
             )
 
     tokens = tokens_ref[...].astype(F32)
-    block_out_ref[...] = (tokens + out_sum_ref[...]).astype(BF16)
+    summed = out_own[...].astype(F32) + out_near[0].astype(F32) + out_far[...].astype(F32)
+    block_out_ref[...] = (tokens + summed).astype(BF16)
     gains = few_ref[...].astype(F32)
     start = sum(sizes) - (sizes[0] + sizes[1])
     gain = jnp.concatenate(
@@ -2186,14 +2295,15 @@
         axis=1,
     )
     scale = lax.rsqrt(jnp.mean(tokens * tokens, axis=-1, keepdims=True) + EPS)
-    scaled = norm_ref[...] * gain
+    summed = norm_own[...].astype(F32) + norm_near[0].astype(F32) + norm_far[...].astype(F32)
+    scaled = summed * gain
     lean = jnp.mean(scaled * tokens, axis=-1, keepdims=True)
     input_grad_ref[...] = (
         grads_ref[...].astype(F32) + scale * scaled - tokens * (scale * scale * scale) * lean
     ).astype(BF16)
 
 
-def place(copy, sizes, inner, gate, out, small, out_sum, norm_sum, tokens, grads, few):
+def place(copy, sizes, inner, gate, out, small, out_terms, norm_terms, tokens, grads, few):
     steps = 4
     _, slab, width = inner.shape
     part, model = out.shape[1:]
@@ -2214,6 +2324,7 @@
     shape = jax.ShapeDtypeStruct
     narrow = [(sizes[0], share), (share, sizes[1]), (sizes[2], share), (sizes[5], share)]
     token_rows = cut_rows(rows, model)
+    near_rows = pl.BlockSpec((1, rows // steps, model), lambda i, copy: (0, i, 0))
     return pl.pallas_call(
         functools.partial(place_kernel, sizes),
         grid_spec=pltpu.PrefetchScalarGridSpec(
@@ -2221,7 +2332,8 @@
             grid=(steps,),
             in_specs=[pieces(slab, width)] * 2
             + [pieces(part, model), fixed(*small.shape)]
-            + [token_rows] * 4
+            + [token_rows, near_rows, token_rows] * 2
+            + [token_rows] * 2
             + [pl.BlockSpec((last, width), lambda i, copy: (first // last, 0))],
             out_specs=[cut_rows(slab, 2 * COPIES * width), pieces(part, model)]
             + [fixed(*n) for n in narrow]
@@ -2238,7 +2350,7 @@
         compiler_params=params(),
         cost_estimate=cost(40 * rows * model, 20 * slab * width),
         name="place",
-    )(copy, inner, gate, out, small, out_sum, norm_sum, tokens, grads, few)
+    )(copy, inner, gate, out, small, *out_terms, *norm_terms, tokens, grads, few)
 
 
 def on_device(
@@ -2320,12 +2432,12 @@
     if fused:
         (
             masks, rate, spread_by, fold_by, normed, cotangent, inner_in, inner, act, act_low, step_low, coef, step,
-            starts, gate, readout, gated, gated_natural, gate_in, out_w,
+            states, gate, readout, gated, gated_natural, gate_in, out_w,
         ) = (
             out[k]
             for k in (
                 "masks", "rate", "spread_by", "fold_by", "normed", "cotangent", "inner_in", "inner", "act", "act_low",
-                "step_low", "coef", "step", "starts", "gate", "readout", "gated", "gated_natural", "gate_in", "out_w",
+                "step_low", "coef", "step", "states", "gate", "readout", "gated", "gated_natural", "gate_in", "out_w",
             )
         )
     else:
@@ -2348,11 +2460,11 @@
         gate = dot(normed, gate_in, 1, 0)
         gated, gated_natural = gate_forward(readout, gate)
     if fused:
-        gate_grad_natural, pre_low, direct, coef_part, sums, *totals = backward(
+        gate_grad_natural, pre_low, direct, coef_part, sums, out_pieces, *out_terms, gate_total = backward(
             fsdp, nstate, rank,
             (
-                gated, cotangent, out_w, readout, gate, normed, step, act, coef, starts, masks, rate, spread_by, fold_by,
-                out["few"],
+                gated, cotangent, out_w, readout, gate, normed, step, act, coef, states, masks, rate, spread_by, fold_by,
+                out["few"], gated_natural,
             ),
         )
     else:
@@ -2368,17 +2480,17 @@
         totals = [scatter.total.astype(BF16) for scatter in scatters]
     small_rows = few.shape[0]
     if fused:
-        inner_pieces, gate_pieces, out_pieces, small_pieces, out_sum, normed_sum = finish(
+        inner_pieces, gate_pieces, *norm_terms, small_pieces = finish(
             fsdp, rank, nstate,
             (
                 pre_low, coef_part, direct, inner, act_low, step_low, masks, out["few"], normed, inner_in, gate_in,
-                gate_grad_natural, gated_natural, out_w, sums, *totals,
+                gate_grad_natural, sums, gate_total,
             ),
             small_rows,
         )
         flat = (batches * length, model)
         entry_all, out_all, select_g, stride_g, taps_g, decay_g, rows_g, block_out, input_grad = place(
-            copy_index, sizes[:-1], inner_pieces, gate_pieces, out_pieces, small_pieces, out_sum, normed_sum,
+            copy_index, sizes[:-1], inner_pieces, gate_pieces, out_pieces, small_pieces, out_terms, norm_terms,
             tokens.reshape(flat), out_grad.reshape(flat), out["few"],
         )
         gain_at = sum(sizes[:-1])

time: 391 us -> 354 us (0.905)
  Pallas kernels: 379 us -> 344 us
    pallas_call x1, Pallas kernels: 115 us -> 92.8 us  [finish(): pl.pallas_call(functools.partial(finish_kernel, size, rank, nstate), in_s...]
    pallas_call x1, Pallas kernels: 150 us -> 142 us  [forward(): pl.pallas_call(functools.partial(forward_kernel, size, rank, nstate), in_...]
    pallas_call x1, Pallas kernels: 103 us -> 98.6 us  [backward(): pl.pallas_call(functools.partial(backward_kernel, size, nstate, rank), in...]
where the time goes in v1:
time: 354 us; the launch traced here: 353 us
  Pallas kernels  344 us (97%)
  local copies, waits for them, and re-layouts  6.8 us (2%)
    pallas_call x1, Pallas kernels, forward(): pl.pallas_call(functools.partial(forward_kernel, size, rank, nstate), in_...  142 us
    pallas_call x1, Pallas kernels, backward(): pl.pallas_call(functools.partial(backward_kernel, size, nstate, rank), in...  98.6 us
    pallas_call x1, Pallas kernels, finish(): pl.pallas_call(functools.partial(finish_kernel, size, rank, nstate), in_s...  92.8 us
    pallas_call x1, Pallas kernels, place(): pl.pallas_call(functools.partial(place_kernel, sizes), grid_spec=pltpu.Pr...  10.8 us

profile of v1, /device:TPU:0, one launch (start us, length us, event | category | flops | bytes accessed | tf_op | source)
XLA Modules:
  0.0 353.0 jit_solution(750917533495180333)
XLA Ops:
  0.6 0.0 copy-start
  0.7 0.8 dynamic-slice_bitcast_fusion.5
  1.5 0.7 dynamic-slice_bitcast_fusion.2
  2.1 0.8 dynamic-slice_bitcast_fusion.3
  2.9 0.7 dynamic-slice_bitcast_fusion.1
  3.6 0.8 constant_dynamic-slice_fusion
  4.4 0.1 copy.26
  4.5 0.0 copy-done
  4.5 0.9 concatenate.3
  5.4 0.6 pad.4.few
  6.1 141.9 %forward.1 = (bf16[320,1024]{1,0:T(8,128)(2,1)}, f32[3,1024,128]{2,1,0:T(8,128)}, f32[16,8,1024]{2,1,0:T(8,128)}, bf16[128,4096]{1,0:T(8,128)(2,1)}, bf16[4096,1...) custom-call(bf16[256,8192]{1,0:T(8,128)(2,1)} %entry.1, ...), custom_call_target="tpu_custom_call" | custom-call | flops 17179869184 | bytes 104857600 | tf_op jit(solution)/shard_map/forward/pallas_call | solution.py:1208
  148.1 98.6 %backward.1 = (bf16[1024,1024]{1,0:T(8,128)(2,1)}, bf16[1024,1024]{1,0:T(8,128)(2,1)}, f32[1024,1024]{1,0:T(8,128)}, f32[1024,128]{1,0:T(8,128)}, f32[18,8,1024]...) custom-call(bf16[1024,1024]{1,0:T(8,128)(2,1)} %get-tuple-element.58, ...), custom_call_target="tpu_custom_call" | custom-call | flops 12884901888 | bytes 209715200 | tf_op jit(solution)/shard_map/backward/pallas_call | solution.py:1785
  246.6 92.8 %finish.1 = (bf16[4,256,1024]{2,1,0:T(8,128)(2,1)}, bf16[4,256,1024]{2,1,0:T(8,128)(2,1)}, bf16[256,2048]{1,0:T(8,128)(2,1)}, bf16[2,256,2048]{2,1,0:T(8,128)(2,...) custom-call(bf16[1024,1024]{1,0:T(8,128)(2,1)} %get-tuple-element.74.pre_low_in, ...), custom_call_target="tpu_custom_call" | custom-call | flops 21474836480 | bytes 104857600 | tf_op jit(solution)/shard_map/finish/pallas_call | solution.py:2230
  339.4 0.7 convert_reduce_fusion
  340.2 0.0 copy-start.2
  340.2 0.0 copy-start.1
  340.2 10.8 %place.1 = (f32[256,8192]{1,0:T(8,128)}, f32[4,128,2048]{2,1,0:T(8,128)}, f32[160,512]{1,0:T(8,128)}, f32[512,128]{1,0:T(8,128)}, f32[4,512]{1,0:T(4,128)}, /*in...) custom-call(s32[1]{0:T(128)} %bitcast.copy_ref, ...), custom_call_target="tpu_custom_call" | custom-call | flops 20971520 | bytes 5242880 | tf_op jit(solution)/shard_map/place/pallas_call | solution.py:2328
  351.0 0.0 copy-done.2
  351.0 0.6 bitcast_divide_fusion
  351.6 1.4 fusion
  353.0 0.0 copy-done.1
  (1 shorter events, 0.0 us)
Async XLA Ops:
  0.6 3.8 %copy-start = (bf16[512,160]{0,1:T(8,128)(2,1)S(1)}, bf16[512,160]{0,1:T(8,128)(2,1)}, u32[]{:S(2)}) copy-start(bf16[512,160]{0,1:T(8,128)(2,1)} %param.20) | copy-start | bytes 491524
  340.2 10.9 %copy-start.2 = (bf16[256]{0:T(256)(128)(2,1)S(1)}, bf16[256]{0:T(256)(128)(2,1)}, u32[]{:S(2)}) copy-start(bf16[256]{0:T(256)(128)(2,1)} %param.16) | copy-start | bytes 1540
  340.2 12.8 %copy-start.1 = (bf16[512,160]{0,1:T(8,128)(2,1)S(1)}, bf16[512,160]{0,1:T(8,128)(2,1)}, u32[]{:S(2)}) copy-start(bf16[512,160]{0,1:T(8,128)(2,1)} %param.20) | copy-start | bytes 491524

commit v2 on v1

--- a/solution.py
+++ b/solution.py
@@ -565,8 +565,8 @@
 
 
 class Parts:
-    def __init__(self, peers, send, sems, parts, near, far, rows):
-        self.peers, self.send, self.sems = peers, send, sems
+    def __init__(self, peers, send, sems, parts, near, far, rows, base=0):
+        self.peers, self.send, self.sems, self.base = peers, send, sems, base
         self.parts, self.near, self.far, self.rows = parts, near, far, rows
 
     def block(self, k):
@@ -574,26 +574,26 @@
 
     def start(self):
         for i in range(2):
-            self.send(self.block(2 * i + 1), self.near.at[i], self.sems, i, self.peers.core)
+            self.send(self.block(2 * i + 1), self.near.at[i], self.sems, self.base + i, self.peers.core)
 
     def come_near(self):
         for i in range(2):
             there = self.near.at[i]
-            remote(there, there, self.sems, i, self.peers.core).wait_recv()
+            remote(there, there, self.sems, self.base + i, self.peers.core).wait_recv()
 
     def go_far(self, here):
         there = self.block(2)
         there[...] = (there[...].astype(F32) + here[...].astype(F32)).astype(BF16)
-        self.send(there, self.far, self.sems, 2, self.peers.across)
+        self.send(there, self.far, self.sems, self.base + 2, self.peers.across)
 
     def come(self):
-        remote(self.far, self.far, self.sems, 2, self.peers.across).wait_recv()
+        remote(self.far, self.far, self.sems, self.base + 2, self.peers.across).wait_recv()
 
     def sent_all(self):
         for i in range(2):
             there = self.near.at[i]
-            remote(there, there, self.sems, i, self.peers.core).wait_send()
-        remote(self.far, self.far, self.sems, 2, self.peers.across).wait_send()
+            remote(there, there, self.sems, self.base + i, self.peers.core).wait_send()
+        remote(self.far, self.far, self.sems, self.base + 2, self.peers.across).wait_send()
 
 
 class Shares:
@@ -1249,7 +1249,7 @@
             return own
         self.copy(which, way, step - 1, c).wait_recv()
         there = self.held[which].at[way, step - 2, self.rows(which, c), :]
-        there[...] = (own[...].astype(F32) + there[...].astype(F32)).astype(BF16)
+        there[...] = own[...] + there[...]
         return there
 
     def step(self, which, step):
@@ -1897,12 +1897,12 @@
     )
     for i in range(2):
         come(got_near.at[i], i, peers.core)
-    to_across[...] = nat[:, 2 * quarter : 3 * quarter, :] + got_near[1]
+    to_across[...] = (nat[:, 2 * quarter : 3 * quarter, :] + got_near[1]).astype(BF16)
     send(to_across, got_across, near, 2, peers.across)
     loads["gate"].wait()
     norm_tiles(w_gate, gate_grad, 0, w_count // 2, False)
     come(got_across, 2, peers.across)
-    mine = nat[:, :quarter, :] + got_near[0] + got_across[...]
+    mine = nat[:, :quarter, :] + got_near[0] + got_across[...].astype(F32)
     for j in range(2):
         shared[0, j] = mine[j].astype(BF16)
     send(shared.at[0], shared.at[2], near, 3, peers.across)
@@ -1979,13 +1979,9 @@
                 if step == 2:
                     here, other = (slice(w * (slab // 2), (w + 1) * (slab // 2)) for w in (way, 1 - way))
                     source[other, :] = wgrad[block_rows(member, 1 - way), cols]
-                    source[here, :] = (
-                        source[here, :].astype(F32) + wgrad[block_rows(member, way), cols].astype(F32)
-                    ).astype(BF16)
+                    source[here, :] = source[here, :] + wgrad[block_rows(member, way), cols]
                 else:
-                    source[...] = (
-                        source[...].astype(F32) + wgrad[block_rows(member), cols].astype(F32)
-                    ).astype(BF16)
+                    source[...] = source[...] + wgrad[block_rows(member), cols]
             send(source, landing(way, step, c), ring_sems, (way, step - 1, c), peers.ring[way])
 
     def fold_rows(value):
@@ -2056,15 +2052,6 @@
         if c >= 2:
             ring_step(2, c - 2)
 
-    loads["sums"].wait()
-    at = first_tap + 5
-    small[at : at + 1, :] = jnp.sum(sums[nstate + 1], axis=0, keepdims=True)
-    for n in range(nstate):
-        small[at + 1 + n : at + 2 + n, :] = LN2 * jnp.sum(sums[n], axis=0, keepdims=True)
-    at = at + 1 + nstate
-    small[at : at + 1, :] = jnp.sum(sums[nstate], axis=0, keepdims=True)
-    small[at + 1 :, :] = jnp.zeros((small.shape[0] - at - 1, width), F32)
-    small_low[...] = small[...].astype(BF16)
     few_half = small.shape[0] // 2
 
     def few_columns(member):
@@ -2096,28 +2083,53 @@
                     source[...] = (source[...].astype(F32) + small_low[:, columns].astype(F32)).astype(BF16)
             send(source, few_landing(way, step), few_sems, (way, step - 1), peers.ring[way])
 
-    norm_sum = Parts(peers, send, (part_send, part_recv), norm_parts, norm_near, norm_far, quarter)
+    half_model = model // 2
+
+    def norm_half(i):
+        cols = pl.ds(i * half_model, half_model)
+        return Parts(
+            peers, send, (part_send, part_recv), norm_parts.at[:, cols], norm_near.at[:, :, cols],
+            norm_far.at[:, cols], quarter, 3 * i,
+        )
+
+    norm_sums = [norm_half(i) for i in range(2)]
+    near_copies = [
+        pltpu.make_async_copy(norm_sums[i].near.at[1], near_at.at[i], w_sems.at[2 + i]) for i in range(2)
+    ]
+    norm_tiles(w_inner, natural, 0, w_count // 2, True)
+    norm_sums[0].start()
+    norm_tiles(w_inner, natural, w_count // 2, w_count - w_count // 2, True)
+    norm_sums[1].start()
+    norm_sums[0].come_near()
+    near_copies[0].start()
+    ring_step(2, 2)
+    near_copies[0].wait()
+    norm_sums[0].go_far(near_at.at[0])
+    norm_sums[1].come_near()
+    near_copies[1].start()
+    ring_step(2, 3)
+    near_copies[1].wait()
+    norm_sums[1].go_far(near_at.at[1])
+
+    loads["sums"].wait()
+    at = first_tap + 5
+    small[at : at + 1, :] = jnp.sum(sums[nstate + 1], axis=0, keepdims=True)
+    for n in range(nstate):
+        small[at + 1 + n : at + 2 + n, :] = LN2 * jnp.sum(sums[n], axis=0, keepdims=True)
+    at = at + 1 + nstate
+    small[at : at + 1, :] = jnp.sum(sums[nstate], axis=0, keepdims=True)
+    small[at + 1 :, :] = jnp.zeros((small.shape[0] - at - 1, width), F32)
+    small_low[...] = small[...].astype(BF16)
     few_step(1)
-    norm_tiles(w_inner, natural, 0, w_count, True)
-    norm_sum.start()
-    ring_step(2, 2)
-    ring_step(2, 3)
-    ring_step(3, 0)
-    norm_sum.come_near()
-    near_copy = pltpu.make_async_copy(norm_near.at[1], near_at, w_sems.at[2])
-    near_copy.start()
-    ring_step(3, 1)
-    near_copy.wait()
-    norm_sum.go_far(near_at)
+    for c in range(tiles):
+        ring_step(3, c)
     few_step(2)
-    ring_step(3, 2)
-    ring_step(3, 3)
     few_step(3)
     own_rows = block_rows(peers.member)
     owns = [
         pltpu.make_async_copy(w_inner.at[own_rows, :], w_tiles.at[0], w_sems.at[0]),
         pltpu.make_async_copy(w_gate.at[own_rows, :], w_tiles.at[1], w_sems.at[1]),
-        pltpu.make_async_copy(norm_sum.block(0), norm_own, w_sems.at[3]),
+        pltpu.make_async_copy(norm_parts.at[pl.ds(0, quarter), :], norm_own, w_sems.at[2]),
     ]
     for copy in owns:
         copy.start()
@@ -2174,7 +2186,8 @@
     small_all.give()
     for pieces in (*inner_all, small_all):
         pieces.pass_on()
-    norm_sum.come()
+    for norm_sum in norm_sums:
+        norm_sum.come()
     for pieces in (gate_all, *inner_all, small_all):
         pieces.come()
     send.wait()
@@ -2198,8 +2211,8 @@
         shape((2, total, LANES), F32),
         shape((2, total, LANES), F32),
         shape((2, 2, quarter, LANES), F32),
-        shape((2, quarter, LANES), F32),
-        shape((2, quarter, LANES), F32),
+        shape((2, quarter, LANES), BF16),
+        shape((2, quarter, LANES), BF16),
         shape((COPIES, 2, quarter, LANES), BF16),
         shape((2, total, LANES), BF16),
         low,
@@ -2218,14 +2231,14 @@
         shape((small_rows, width), BF16),
         shape((2, half, small_rows, LANES), BF16),
         wide,
-        part,
+        shape((2, quarter, model // 2), BF16),
         shape((2, 256, width), BF16),
         shape((slab, width), BF16),
         shape((slab, width), BF16),
         shape(sums.shape, F32),
     ]
     tiles = width // 256
-    sems = [(10,), (2, 2), (4,)] + [(6,)] * 2 + [(3,)] * 2 + [(2, half, tiles)] * 2 + [(2, half)] * 2
+    sems = [(10,), (2, 2), (4,)] + [(6,)] * 2 + [(6,)] * 2 + [(2, half, tiles)] * 2 + [(2, half)] * 2
     sems += [(2 + tiles, 3)] * 2 + [(1 + tiles,)]
     return pl.pallas_call(
         functools.partial(finish_kernel, size, rank, nstate),
@@ -2304,7 +2317,7 @@
 
 
 def place(copy, sizes, inner, gate, out, small, out_terms, norm_terms, tokens, grads, few):
-    steps = 4
+    steps = 2
     _, slab, width = inner.shape
     part, model = out.shape[1:]
     rows = tokens.shape[0]

time: 354 us -> 352 us (level)
  no operation moved by 1% of the time
where the time goes in v2:
time: 352 us; the launch traced here: 351 us
  Pallas kernels  342 us (97%)
  local copies, waits for them, and re-layouts  6.8 us (2%)
    pallas_call x1, Pallas kernels, forward(): pl.pallas_call(functools.partial(forward_kernel, size, rank, nstate), in_...  142 us
    pallas_call x1, Pallas kernels, backward(): pl.pallas_call(functools.partial(backward_kernel, size, nstate, rank), in...  98.4 us
    pallas_call x1, Pallas kernels, finish(): pl.pallas_call(functools.partial(finish_kernel, size, rank, nstate), in_s...  91.5 us
    pallas_call x1, Pallas kernels, place(): pl.pallas_call(functools.partial(place_kernel, sizes), grid_spec=pltpu.Pr...  9.98 us

profile of v2, /device:TPU:0, one launch (start us, length us, event | category | flops | bytes accessed | tf_op | source)
XLA Modules:
  0.0 350.7 jit_solution(17780108852352103718)
XLA Ops:
  0.6 0.0 copy-start
  0.7 0.8 dynamic-slice_bitcast_fusion.5
  1.5 0.7 dynamic-slice_bitcast_fusion.2
  2.1 0.8 dynamic-slice_bitcast_fusion.3
  2.9 0.7 dynamic-slice_bitcast_fusion.1
  3.6 0.8 constant_dynamic-slice_fusion
  4.4 0.1 copy.26
  4.5 0.0 copy-done
  4.5 0.9 concatenate.3
  5.4 0.6 pad.4.few
  6.1 141.9 %forward.1 = (bf16[320,1024]{1,0:T(8,128)(2,1)}, f32[3,1024,128]{2,1,0:T(8,128)}, f32[16,8,1024]{2,1,0:T(8,128)}, bf16[128,4096]{1,0:T(8,128)(2,1)}, bf16[4096,1...) custom-call(bf16[256,8192]{1,0:T(8,128)(2,1)} %entry.1, ...), custom_call_target="tpu_custom_call" | custom-call | flops 17179869184 | bytes 104857600 | tf_op jit(solution)/shard_map/forward/pallas_call | solution.py:1208
  148.1 98.4 %backward.1 = (bf16[1024,1024]{1,0:T(8,128)(2,1)}, bf16[1024,1024]{1,0:T(8,128)(2,1)}, f32[1024,1024]{1,0:T(8,128)}, f32[1024,128]{1,0:T(8,128)}, f32[18,8,1024]...) custom-call(bf16[1024,1024]{1,0:T(8,128)(2,1)} %get-tuple-element.58, ...), custom_call_target="tpu_custom_call" | custom-call | flops 12884901888 | bytes 209715200 | tf_op jit(solution)/shard_map/backward/pallas_call | solution.py:1785
  246.5 91.5 %finish.1 = (bf16[4,256,1024]{2,1,0:T(8,128)(2,1)}, bf16[4,256,1024]{2,1,0:T(8,128)(2,1)}, bf16[256,2048]{1,0:T(8,128)(2,1)}, bf16[2,256,2048]{2,1,0:T(8,128)(2,...) custom-call(bf16[1024,1024]{1,0:T(8,128)(2,1)} %get-tuple-element.74.pre_low_in, ...), custom_call_target="tpu_custom_call" | custom-call | flops 21474836480 | bytes 104857600 | tf_op jit(solution)/shard_map/finish/pallas_call | solution.py:2243
  338.0 0.7 convert_reduce_fusion
  338.7 0.0 copy-start.2
  338.7 0.0 copy-start.1
  338.7 10.0 %place.1 = (f32[256,8192]{1,0:T(8,128)}, f32[4,128,2048]{2,1,0:T(8,128)}, f32[160,512]{1,0:T(8,128)}, f32[512,128]{1,0:T(8,128)}, f32[4,512]{1,0:T(4,128)}, /*in...) custom-call(s32[1]{0:T(128)} %bitcast.copy_ref, ...), custom_call_target="tpu_custom_call" | custom-call | flops 20971520 | bytes 5242880 | tf_op jit(solution)/shard_map/place/pallas_call | solution.py:2341
  348.7 0.0 copy-done.2
  348.7 0.6 bitcast_divide_fusion
  349.3 1.4 fusion
  350.7 0.0 copy-done.1
  (1 shorter events, 0.0 us)
Async XLA Ops:
  0.6 3.8 %copy-start = (bf16[512,160]{0,1:T(8,128)(2,1)S(1)}, bf16[512,160]{0,1:T(8,128)(2,1)}, u32[]{:S(2)}) copy-start(bf16[512,160]{0,1:T(8,128)(2,1)} %param.20) | copy-start | bytes 491524
  338.7 10.0 %copy-start.2 = (bf16[256]{0:T(256)(128)(2,1)S(1)}, bf16[256]{0:T(256)(128)(2,1)}, u32[]{:S(2)}) copy-start(bf16[256]{0:T(256)(128)(2,1)} %param.16) | copy-start | bytes 1540
  338.7 12.0 %copy-start.1 = (bf16[512,160]{0,1:T(8,128)(2,1)S(1)}, bf16[512,160]{0,1:T(8,128)(2,1)}, u32[]{:S(2)}) copy-start(bf16[512,160]{0,1:T(8,128)(2,1)} %param.20) | copy-start | bytes 491524
